TPU v7x, 32 devices: a whole 2x2x4 slice. The times are simulated.
32 devices in a mesh: dom: 8 (over z, x), blk: 4 (over y, core).
Axes of the slice: x: 2, y: 2, z: 4, core: 2. Of those that a mesh axis runs over, the one named last changes fastest.
Arguments:
- degree: int32 [64], P('dom'), may hold values from 1 to 3
- face_elem: int32 [256], P('dom'), may hold values from 0 to 7
- face_side: int32 [256], P('dom'), may hold values from 0 to 8, as said below
- face_peer: int32 [256], P('dom'), may hold values from 0 to 7
- coupling: bfloat16 [256, 320, 320], P('dom', 'blk'), may hold values from -0.078125 to 0.078125
- inv_diag: float32 [64, 320], P('dom', 'blk'), may hold values from 0.5 to 2
- inv_off: bfloat16 [64, 320, 320], P('dom', 'blk'), may hold values from -0.109375 to 0.109375
- source: float32 [64, 320], P('dom', 'blk'), may hold values from -6 to 6
- residual: float32 [64, 320], P('dom', 'blk'), may hold values from -0.6 to 0.6
Outputs:
- adjoint: float32 [64, 320], P('dom', 'blk')
- indicator: float32 [64], P('dom')
Inputs may be any that keep to these rules, and one draw needn't show every extreme that they name: `face_side`: among the 32 faces of one partition (aligned blocks of 32 rows) each side from 1 to 8 is named by at least 2 and at most 4 faces, and one side by exactly 4; the remaining faces have side 0.
All inputs are finite; a program needn't handle non-finite values.
Results may differ from a plain program's by a relative error of at most 0.004.
Values may be sent and summed in bfloat16 or wider, within the bound.
A program may use at most 64 MiB of HBM per device.

v0:
```python
import jax
import jax.numpy as jnp
from jax import lax
from jax.sharding import PartitionSpec as P

MODES = 64
SWEEPS = 2
NEIGH = 8


def from_behind(block, axis, distance):
    devices = range(lax.axis_size(axis))
    route = [((i - distance) % len(devices), i) for i in devices]
    return lax.ppermute(block, axis, route)


def full_rows(values):
    return lax.all_gather(values, "blk", axis=1, tiled=True)


def local(degree, face_elem, face_side, face_peer, coupling, inv_diag, inv_off, source, residual):
    width = coupling.shape[2]
    quarter = source.shape[1]
    elements = source.shape[0]
    faces = coupling.shape[0]
    neigh = NEIGH
    half_count = neigh // 2
    capacity = faces // neigh
    offsets = [step_size for step_size in range(1, half_count + 1)] + [
        -step_size for step_size in range(1, half_count + 1)
    ]
    first_row = lax.axis_index("blk") * quarter
    limit = (degree + 1) ** 3 * MODES // 64
    modes = jnp.arange(width, dtype=jnp.int32) % MODES
    mask_full = (modes[None, :] < limit[:, None]).astype(jnp.float32)
    mask_rows = lax.dynamic_slice_in_dim(mask_full, first_row, quarter, 1)
    codes = jnp.arange(neigh + 1, dtype=jnp.int32)
    onehot = (face_side[:, None] == codes[None, :]).astype(jnp.int32)
    before = jnp.cumsum(onehot, axis=0) - onehot
    slot_index = jnp.sum(before * onehot, axis=1)
    crossing = face_side > 0
    inner = jnp.where(crossing, 0.0, 1.0).astype(jnp.float32)
    position = jnp.where(crossing, (face_side - 1) * capacity + slot_index, neigh * capacity)
    safe_position = jnp.minimum(position, neigh * capacity - 1)
    wanted = (
        jnp.zeros((neigh * capacity,), jnp.int32)
        .at[position]
        .set(face_peer, mode="drop")
        .reshape(neigh, capacity)
    )
    requested = jnp.stack(
        [from_behind(wanted[side_num], "dom", offsets[side_num]) for side_num in range(neigh)]
    )
    requested_flat = requested.reshape(-1)

    def invert(values_full):
        own_part = lax.dynamic_slice_in_dim(values_full, first_row, quarter, 1)
        product = jnp.einsum("eij,ej->ei", inv_off, values_full, preferred_element_type=jnp.float32)
        return inv_diag * own_part.astype(jnp.float32) + product

    source_half = (source * mask_rows).astype(jnp.bfloat16)
    base_state = invert(full_rows(source_half)) * mask_rows
    adjoint = base_state
    for sweep_index in range(SWEEPS):
        state_rows = adjoint.astype(jnp.bfloat16)
        state_full = full_rows(state_rows)
        outgoing = state_full[requested]
        incoming = jnp.stack(
            [
                from_behind(outgoing[side_num], "dom", -offsets[side_num])
                for side_num in range(neigh)
            ]
        ).reshape(-1, width)
        peer_state = jnp.where(crossing[:, None], incoming[safe_position], state_full[face_peer])
        elem_state = state_rows[face_elem]
        local_terms = jnp.einsum(
            "fij,fj->fi", coupling, peer_state, preferred_element_type=jnp.float32
        )
        transposed = jnp.einsum(
            "fij,fi->fj", coupling, elem_state, preferred_element_type=jnp.float32
        )
        own_terms = jnp.zeros((elements, quarter), jnp.float32).at[face_elem].add(local_terms)
        shares = lax.psum_scatter(transposed, "blk", scatter_dimension=1, tiled=True)
        row_terms = own_terms + jnp.zeros((elements, quarter), jnp.float32).at[face_peer].add(
            shares * inner[:, None]
        )
        outbound = (
            jnp.zeros((neigh * capacity, quarter), jnp.float32)
            .at[position]
            .set(shares, mode="drop")
            .reshape(neigh, capacity, quarter)
        )
        returned = jnp.stack(
            [from_behind(outbound[side_num], "dom", offsets[side_num]) for side_num in range(neigh)]
        ).reshape(-1, quarter)
        row_terms = row_terms.at[requested_flat].add(returned)
        coupled_half = lax.all_gather(
            (row_terms * mask_rows).astype(jnp.bfloat16), "blk", axis=1, tiled=True
        )
        adjoint = (base_state - invert(coupled_half)) * mask_rows
    weights = jnp.sum(adjoint * residual * mask_rows, axis=1)
    indicator = lax.psum(weights, "blk")
    return (adjoint, indicator)


def solution(mesh):
    in_specs = (
        P("dom"),
        P("dom"),
        P("dom"),
        P("dom"),
        P("dom", "blk", None),
        P("dom", "blk"),
        P("dom", "blk", None),
        P("dom", "blk"),
        P("dom", "blk"),
    )
    out_specs = (P("dom", "blk"), P("dom"))
    return jax.shard_map(local, mesh=mesh, in_specs=in_specs, out_specs=out_specs, check_vma=False)
```

profile of v0, /device:TPU:0, one launch (start us, length us, event | category | flops | bytes accessed | tf_op | source)
XLA Modules:
  0.0 154.7 jit_solution(16112179411258452085)
XLA Ops:
  8.9 6.1 %all-gather = bf16[4,80,8]{1,2,0:T(8,128)(2,1)S(1)} all-gather(bf16[1,80,8]{1,2,0:T(8,128)(2,1)S(1)} %fusion.38), channel_id=1, replica_groups=mesh['dom'=8,'blk'=4] {'blk'}, dimensions={0}, use_global_device_ids=true | all-gather | bytes 6400 | tf_op jit(solution)/shard_map/all_gather | solution.py:18
  15.8 1.3 fusion.17
  20.9 2.0 %collective-permute-start = (s32[4]{0:T(128)S(1)}, s32[4]{0:T(128)S(1)}, u32[]{:S(2)}, u32[]{:S(2)}) collective-permute-start(s32[4]{0:T(128)S(1)} %get-tuple-element.45), channel_id=1, source_target_pairs={{28,0},{0,4},{4,8},{8,12},{12,16},{16,20},{20,24},{24,28},{29,1},{... | collective-permute-start | bytes 56 | tf_op jit(solution)/shard_map/ppermute | solution.py:14
  22.9 1.6 %collective-permute-start.1 = (s32[4]{0:T(128)S(1)}, s32[4]{0:T(128)S(1)}, u32[]{:S(2)}, u32[]{:S(2)}) collective-permute-start(s32[4]{0:T(128)S(1)} %get-tuple-element.44), channel_id=1, source_target_pairs={{24,0},{28,4},{0,8},{4,12},{8,16},{12,20},{16,24},{20,28},{25,1},{... | collective-permute-start | bytes 56 | tf_op jit(solution)/shard_map/ppermute | solution.py:14
  24.4 2.6 %collective-permute-start.2 = (s32[4]{0:T(128)S(1)}, s32[4]{0:T(128)S(1)}, u32[]{:S(2)}, u32[]{:S(2)}) collective-permute-start(s32[4]{0:T(128)S(1)} %get-tuple-element.43), channel_id=1, source_target_pairs={{20,0},{24,4},{28,8},{0,12},{4,16},{8,20},{12,24},{16,28},{21,1},{... | collective-permute-start | bytes 56 | tf_op jit(solution)/shard_map/ppermute | solution.py:14
  27.0 1.2 collective-permute-start.3
  28.2 2.3 %collective-permute-start.4 = (s32[4]{0:T(128)S(1)}, s32[4]{0:T(128)S(1)}, u32[]{:S(2)}, u32[]{:S(2)}) collective-permute-start(s32[4]{0:T(128)S(1)} %get-tuple-element.41), channel_id=1, source_target_pairs={{4,0},{8,4},{12,8},{16,12},{20,16},{24,20},{28,24},{0,28},{5,1},{9... | collective-permute-start | bytes 56 | tf_op jit(solution)/shard_map/ppermute | solution.py:14
  30.5 5.2 %all-gather.1 = bf16[4,80,8]{1,2,0:T(8,128)(2,1)S(1)} all-gather(bf16[1,80,8]{1,2,0:T(8,128)(2,1)S(1)} %bitcast.198), channel_id=1, replica_groups=mesh['dom'=8,'blk'=4] {'blk'}, dimensions={0}, use_global_device_ids=true | all-gather | bytes 6400 | tf_op jit(solution)/shard_map/all_gather | solution.py:18
  36.5 1.9 %collective-permute-start.5 = (s32[4]{0:T(128)S(1)}, s32[4]{0:T(128)S(1)}, u32[]{:S(2)}, u32[]{:S(2)}) collective-permute-start(s32[4]{0:T(128)S(1)} %get-tuple-element.40), channel_id=1, source_target_pairs={{8,0},{12,4},{16,8},{20,12},{24,16},{28,20},{0,24},{4,28},{9,1},{1... | collective-permute-start | bytes 56 | tf_op jit(solution)/shard_map/ppermute | solution.py:14
  38.7 1.1 collective-permute-start.7
  40.1 2.7 %collective-permute-done.6 = s32[4]{0:T(128)S(1)} collective-permute-done((s32[4]{0:T(128)S(1)}, s32[4]{0:T(128)S(1)}, u32[]{:S(2)}, u32[]{:S(2)}) %collective-permute-start.6) | collective-permute-done | bytes 48 | tf_op jit(solution)/shard_map/ppermute | solution.py:14
  44.0 2.0 %collective-permute-start.8 = (bf16[4,320]{1,0:T(4,128)(2,1)S(1)}, bf16[4,320]{1,0:T(4,128)(2,1)S(1)}, u32[]{:S(2)}, u32[]{:S(2)}) collective-permute-start(bf16[4,320]{1,0:T(4,128)(2,1)S(1)} %get-tuple-element.21), channel_id=1, source_target_pairs={{4,0},{8,4},{12,8},{16,12},{20,16},{24,20},{28,24},{0,28},{5,1},{9... | collective-permute-start | bytes 7688 | tf_op jit(solution)/shard_map/ppermute | solution.py:14
  46.0 1.7 %collective-permute-start.9 = (bf16[4,320]{1,0:T(4,128)(2,1)S(1)}, bf16[4,320]{1,0:T(4,128)(2,1)S(1)}, u32[]{:S(2)}, u32[]{:S(2)}) collective-permute-start(bf16[4,320]{1,0:T(4,128)(2,1)S(1)} %get-tuple-element.20), channel_id=1, source_target_pairs={{8,0},{12,4},{16,8},{20,12},{24,16},{28,20},{0,24},{4,28},{9,1},{1... | collective-permute-start | bytes 7688 | tf_op jit(solution)/shard_map/ppermute | solution.py:14
  48.0 2.2 %collective-permute-start.11 = (bf16[4,320]{1,0:T(4,128)(2,1)S(1)}, bf16[4,320]{1,0:T(4,128)(2,1)S(1)}, u32[]{:S(2)}, u32[]{:S(2)}) collective-permute-start(bf16[4,320]{1,0:T(4,128)(2,1)S(1)} %get-tuple-element.18), channel_id=1, source_target_pairs={{16,0},{20,4},{24,8},{28,12},{0,16},{4,20},{8,24},{12,28},{17,1},{... | collective-permute-start | bytes 7688 | tf_op jit(solution)/shard_map/ppermute | solution.py:14
  51.0 1.1 collective-permute-start.13
  52.1 1.9 %collective-permute-start.14 = (bf16[4,320]{1,0:T(4,128)(2,1)S(1)}, bf16[4,320]{1,0:T(4,128)(2,1)S(1)}, u32[]{:S(2)}, u32[]{:S(2)}) collective-permute-start(bf16[4,320]{1,0:T(4,128)(2,1)S(1)} %get-tuple-element.15), channel_id=1, source_target_pairs={{20,0},{24,4},{28,8},{0,12},{4,16},{8,20},{12,24},{16,28},{21,1},{... | collective-permute-start | bytes 7688 | tf_op jit(solution)/shard_map/ppermute | solution.py:14
  54.0 1.9 %collective-permute-start.15 = (bf16[4,320]{1,0:T(4,128)(2,1)S(1)}, bf16[4,320]{1,0:T(4,128)(2,1)S(1)}, u32[]{:S(2)}, u32[]{:S(2)}) collective-permute-start(bf16[4,320]{1,0:T(4,128)(2,1)S(1)} %get-tuple-element.14), channel_id=1, source_target_pairs={{16,0},{20,4},{24,8},{28,12},{0,16},{4,20},{8,24},{12,28},{17,1},{... | collective-permute-start | bytes 7688 | tf_op jit(solution)/shard_map/ppermute | solution.py:14
  56.5 0.9 collective-permute-done.14
  57.5 1.1 collective-permute-done.15
  59.4 0.8 copy.37
  60.9 1.7 %collective-permute-start.16 = (f32[4,80]{1,0:T(4,128)S(1)}, f32[4,80]{1,0:T(4,128)S(1)}, u32[]{:S(2)}, u32[]{:S(2)}) collective-permute-start(f32[4,80]{1,0:T(4,128)S(1)} %get-tuple-element.37), channel_id=1, source_target_pairs={{28,0},{0,4},{4,8},{8,12},{12,16},{16,20},{20,24},{24,28},{29,1},{... | collective-permute-start | bytes 3848 | tf_op jit(solution)/shard_map/ppermute | solution.py:14
  64.1 1.3 collective-permute-start.17
  65.4 1.5 collective-permute-start.18
  67.0 3.1 %collective-permute-start.19 = (f32[4,80]{1,0:T(4,128)S(1)}, f32[4,80]{1,0:T(4,128)S(1)}, u32[]{:S(2)}, u32[]{:S(2)}) collective-permute-start(f32[4,80]{1,0:T(4,128)S(1)} %get-tuple-element.34), channel_id=1, source_target_pairs={{16,0},{20,4},{24,8},{28,12},{0,16},{4,20},{8,24},{12,28},{17,1},{... | collective-permute-start | bytes 3848 | tf_op jit(solution)/shard_map/ppermute | solution.py:14
  70.0 1.8 %collective-permute-start.20 = (f32[4,80]{1,0:T(4,128)S(1)}, f32[4,80]{1,0:T(4,128)S(1)}, u32[]{:S(2)}, u32[]{:S(2)}) collective-permute-start(f32[4,80]{1,0:T(4,128)S(1)} %get-tuple-element.33), channel_id=1, source_target_pairs={{4,0},{8,4},{12,8},{16,12},{20,16},{24,20},{28,24},{0,28},{5,1},{9... | collective-permute-start | bytes 3848 | tf_op jit(solution)/shard_map/ppermute | solution.py:14
  72.6 1.0 collective-permute-start.21
  74.0 1.9 %collective-permute-start.23 = (f32[4,80]{1,0:T(4,128)S(1)}, f32[4,80]{1,0:T(4,128)S(1)}, u32[]{:S(2)}, u32[]{:S(2)}) collective-permute-start(f32[4,80]{1,0:T(4,128)S(1)} %get-tuple-element.30), channel_id=1, source_target_pairs={{16,0},{20,4},{24,8},{28,12},{0,16},{4,20},{8,24},{12,28},{17,1},{... | collective-permute-start | bytes 3848 | tf_op jit(solution)/shard_map/ppermute | solution.py:14
  76.3 1.8 %collective-permute-done.22 = f32[4,80]{1,0:T(4,128)S(1)} collective-permute-done((f32[4,80]{1,0:T(4,128)S(1)}, f32[4,80]{1,0:T(4,128)S(1)}, u32[]{:S(2)}, u32[]{:S(2)}) %collective-permute-start.22) | collective-permute-done | bytes 1312 | tf_op jit(solution)/shard_map/ppermute | solution.py:14
  79.3 5.2 %all-gather.2 = bf16[4,80,8]{1,2,0:T(8,128)(2,1)S(1)} all-gather(bf16[1,80,8]{1,2,0:T(8,128)(2,1)S(1)} %fusion.37), channel_id=1, replica_groups=mesh['dom'=8,'blk'=4] {'blk'}, dimensions={0}, use_global_device_ids=true | all-gather | bytes 6400 | tf_op jit(solution)/shard_map/all_gather | solution.py:97
  85.5 5.2 %all-gather.3 = bf16[4,80,8]{1,2,0:T(8,128)(2,1)S(1)} all-gather(bf16[1,80,8]{1,2,0:T(8,128)(2,1)S(1)} %bitcast.199), channel_id=1, replica_groups=mesh['dom'=8,'blk'=4] {'blk'}, dimensions={0}, use_global_device_ids=true | all-gather | bytes 6400 | tf_op jit(solution)/shard_map/all_gather | solution.py:18
  91.4 2.0 %collective-permute-start.24 = (bf16[4,320]{1,0:T(4,128)(2,1)S(1)}, bf16[4,320]{1,0:T(4,128)(2,1)S(1)}, u32[]{:S(2)}, u32[]{:S(2)}) collective-permute-start(bf16[4,320]{1,0:T(4,128)(2,1)S(1)} %get-tuple-element.13), channel_id=1, source_target_pairs={{4,0},{8,4},{12,8},{16,12},{20,16},{24,20},{28,24},{0,28},{5,1},{9... | collective-permute-start | bytes 7688 | tf_op jit(solution)/shard_map/ppermute | solution.py:14
  95.4 2.6 %collective-permute-start.25 = (bf16[4,320]{1,0:T(4,128)(2,1)S(1)}, bf16[4,320]{1,0:T(4,128)(2,1)S(1)}, u32[]{:S(2)}, u32[]{:S(2)}) collective-permute-start(bf16[4,320]{1,0:T(4,128)(2,1)S(1)} %get-tuple-element.12), channel_id=1, source_target_pairs={{8,0},{12,4},{16,8},{20,12},{24,16},{28,20},{0,24},{4,28},{9,1},{1... | collective-permute-start | bytes 7688 | tf_op jit(solution)/shard_map/ppermute | solution.py:14
  98.0 2.6 %collective-permute-start.27 = (bf16[4,320]{1,0:T(4,128)(2,1)S(1)}, bf16[4,320]{1,0:T(4,128)(2,1)S(1)}, u32[]{:S(2)}, u32[]{:S(2)}) collective-permute-start(bf16[4,320]{1,0:T(4,128)(2,1)S(1)} %get-tuple-element.10), channel_id=1, source_target_pairs={{16,0},{20,4},{24,8},{28,12},{0,16},{4,20},{8,24},{12,28},{17,1},{... | collective-permute-start | bytes 7688 | tf_op jit(solution)/shard_map/ppermute | solution.py:14
  100.6 0.9 collective-permute-start.29
  101.5 1.8 %collective-permute-start.30 = (bf16[4,320]{1,0:T(4,128)(2,1)S(1)}, bf16[4,320]{1,0:T(4,128)(2,1)S(1)}, u32[]{:S(2)}, u32[]{:S(2)}) collective-permute-start(bf16[4,320]{1,0:T(4,128)(2,1)S(1)} %get-tuple-element.7), channel_id=1, source_target_pairs={{20,0},{24,4},{28,8},{0,12},{4,16},{8,20},{12,24},{16,28},{21,1},{... | collective-permute-start | bytes 7688 | tf_op jit(solution)/shard_map/ppermute | solution.py:14
  103.3 2.7 %collective-permute-start.31 = (bf16[4,320]{1,0:T(4,128)(2,1)S(1)}, bf16[4,320]{1,0:T(4,128)(2,1)S(1)}, u32[]{:S(2)}, u32[]{:S(2)}) collective-permute-start(bf16[4,320]{1,0:T(4,128)(2,1)S(1)} %get-tuple-element.6), channel_id=1, source_target_pairs={{16,0},{20,4},{24,8},{28,12},{0,16},{4,20},{8,24},{12,28},{17,1},{... | collective-permute-start | bytes 7688 | tf_op jit(solution)/shard_map/ppermute | solution.py:14
  108.6 5.9 %reduce-scatter.9.cloned.1.call-done = f32[80,32]{1,0:T(8,128)} async-done(((f32[320,32]{1,0:T(8,128)}), f32[80,32]{1,0:T(8,128)}) %reduce-scatter.9.cloned.1.call-update) | async-done | bytes 10256
  114.5 0.8 copy.39
  116.0 1.5 collective-permute-start.32
  119.8 1.5 collective-permute-start.33
  121.4 2.4 %collective-permute-start.34 = (f32[4,80]{1,0:T(4,128)S(1)}, f32[4,80]{1,0:T(4,128)S(1)}, u32[]{:S(2)}, u32[]{:S(2)}) collective-permute-start(f32[4,80]{1,0:T(4,128)S(1)} %get-tuple-element.27), channel_id=1, source_target_pairs={{20,0},{24,4},{28,8},{0,12},{4,16},{8,20},{12,24},{16,28},{21,1},{... | collective-permute-start | bytes 3848 | tf_op jit(solution)/shard_map/ppermute | solution.py:14
  123.8 1.4 collective-permute-start.35
  125.2 2.4 %collective-permute-start.36 = (f32[4,80]{1,0:T(4,128)S(1)}, f32[4,80]{1,0:T(4,128)S(1)}, u32[]{:S(2)}, u32[]{:S(2)}) collective-permute-start(f32[4,80]{1,0:T(4,128)S(1)} %get-tuple-element.25), channel_id=1, source_target_pairs={{4,0},{8,4},{12,8},{16,12},{20,16},{24,20},{28,24},{0,28},{5,1},{9... | collective-permute-start | bytes 3848 | tf_op jit(solution)/shard_map/ppermute | solution.py:14
  127.6 1.5 collective-permute-start.37
  129.6 1.4 collective-permute-start.39
  131.2 2.4 %collective-permute-done.38 = f32[4,80]{1,0:T(4,128)S(1)} collective-permute-done((f32[4,80]{1,0:T(4,128)S(1)}, f32[4,80]{1,0:T(4,128)S(1)}, u32[]{:S(2)}, u32[]{:S(2)}) %collective-permute-start.38) | collective-permute-done | bytes 1312 | tf_op jit(solution)/shard_map/ppermute | solution.py:14
  134.9 5.2 %all-gather.4 = bf16[4,80,8]{1,2,0:T(8,128)(2,1)S(1)} all-gather(bf16[1,80,8]{1,2,0:T(8,128)(2,1)S(1)} %fusion.36), channel_id=1, replica_groups=mesh['dom'=8,'blk'=4] {'blk'}, dimensions={0}, use_global_device_ids=true | all-gather | bytes 6400 | tf_op jit(solution)/shard_map/all_gather | solution.py:97
  141.2 6.6 %psum.7 = f32[8]{0:T(128)} all-reduce(f32[8]{0:T(128)S(1)} %get-tuple-element.2), channel_id=1, replica_groups=mesh['dom'=8,'blk'=4] {'blk'}, use_global_device_ids=true, to_apply=%region_14.15 | all-reduce | flops 8 | bytes 64 | tf_op jit(solution)/shard_map/psum | solution.py:102
  (172 shorter events, 28.7 us)
Async XLA Ops:
  7.2 11.3 %copy-start = (bf16[32,80,320]{2,1,0:T(8,128)(2,1)S(1)}, bf16[32,80,320]{2,1,0:T(8,128)(2,1)}, u32[]{:S(2)}) copy-start(bf16[32,80,320]{2,1,0:T(8,128)(2,1)} %param.13) | copy-start | bytes 4915204
  7.2 12.6 %copy-start.2 = (s32[32]{0:T(128)S(1)}, s32[32]{0:T(128)}, u32[]{:S(2)}) copy-start(s32[32]{0:T(128)} %param.11) | copy-start | bytes 388
  7.2 12.9 %copy-start.5 = (s32[32]{0:T(128)S(1)}, s32[32]{0:T(128)}, u32[]{:S(2)}) copy-start(s32[32]{0:T(128)} %param.12) | copy-start | bytes 388
  7.2 52.2 %reduce-scatter.7.cloned.1.call-start = ((), (), s32[]{:S(2)}) async-start(), calls=%async_computation.2 | async-start | bytes 204800
  19.7 64.9 %copy-start.4 = (bf16[8,80,320]{2,1,0:T(8,128)(2,1)S(1)}, bf16[8,80,320]{2,1,0:T(8,128)(2,1)}, u32[]{:S(2)}) copy-start(bf16[8,80,320]{2,1,0:T(8,128)(2,1)} %param.15) | copy-start | bytes 1228804
  19.7 94.8 %reduce-scatter.9.cloned.1.call-start = ((), (), s32[]{:S(2)}) async-start(), calls=%async_computation.3 | async-start | bytes 204800
  20.9 15.6 %collective-permute-start = (s32[4]{0:T(128)S(1)}, s32[4]{0:T(128)S(1)}, u32[]{:S(2)}, u32[]{:S(2)}) collective-permute-start(s32[4]{0:T(128)S(1)} %get-tuple-element.45), channel_id=1, source_target_pairs={{28,0},{0,4},{4,8},{8,12},{12,16},{16,20},{20,24},{24,28},{29,1},{... | collective-permute-start | bytes 56 | tf_op jit(solution)/shard_map/ppermute | solution.py:14
  22.9 15.5 %collective-permute-start.1 = (s32[4]{0:T(128)S(1)}, s32[4]{0:T(128)S(1)}, u32[]{:S(2)}, u32[]{:S(2)}) collective-permute-start(s32[4]{0:T(128)S(1)} %get-tuple-element.44), channel_id=1, source_target_pairs={{24,0},{28,4},{0,8},{4,12},{8,16},{12,20},{16,24},{20,28},{25,1},{... | collective-permute-start | bytes 56 | tf_op jit(solution)/shard_map/ppermute | solution.py:14
  24.4 14.3 %collective-permute-start.2 = (s32[4]{0:T(128)S(1)}, s32[4]{0:T(128)S(1)}, u32[]{:S(2)}, u32[]{:S(2)}) collective-permute-start(s32[4]{0:T(128)S(1)} %get-tuple-element.43), channel_id=1, source_target_pairs={{20,0},{24,4},{28,8},{0,12},{4,16},{8,20},{12,24},{16,28},{21,1},{... | collective-permute-start | bytes 56 | tf_op jit(solution)/shard_map/ppermute | solution.py:14
  27.0 12.9 %collective-permute-start.3 = (s32[4]{0:T(128)S(1)}, s32[4]{0:T(128)S(1)}, u32[]{:S(2)}, u32[]{:S(2)}) collective-permute-start(s32[4]{0:T(128)S(1)} %get-tuple-element.42), channel_id=1, source_target_pairs={{16,0},{20,4},{24,8},{28,12},{0,16},{4,20},{8,24},{12,28},{17,1},{... | collective-permute-start | bytes 56 | tf_op jit(solution)/shard_map/ppermute | solution.py:14
  28.2 11.6 %collective-permute-start.4 = (s32[4]{0:T(128)S(1)}, s32[4]{0:T(128)S(1)}, u32[]{:S(2)}, u32[]{:S(2)}) collective-permute-start(s32[4]{0:T(128)S(1)} %get-tuple-element.41), channel_id=1, source_target_pairs={{4,0},{8,4},{12,8},{16,12},{20,16},{24,20},{28,24},{0,28},{5,1},{9... | collective-permute-start | bytes 56 | tf_op jit(solution)/shard_map/ppermute | solution.py:14
  36.4 48.4 %copy-start.1 = (f32[8,80]{1,0:T(8,128)S(1)}, f32[8,80]{1,0:T(8,128)}, u32[]{:S(2)}) copy-start(f32[8,80]{1,0:T(8,128)} %param.14) | copy-start | bytes 7684
  36.5 3.6 %collective-permute-start.5 = (s32[4]{0:T(128)S(1)}, s32[4]{0:T(128)S(1)}, u32[]{:S(2)}, u32[]{:S(2)}) collective-permute-start(s32[4]{0:T(128)S(1)} %get-tuple-element.40), channel_id=1, source_target_pairs={{8,0},{12,4},{16,8},{20,12},{24,16},{28,20},{0,24},{4,28},{9,1},{1... | collective-permute-start | bytes 56 | tf_op jit(solution)/shard_map/ppermute | solution.py:14
  38.3 4.4 %collective-permute-start.6 = (s32[4]{0:T(128)S(1)}, s32[4]{0:T(128)S(1)}, u32[]{:S(2)}, u32[]{:S(2)}) collective-permute-start(s32[4]{0:T(128)S(1)} %get-tuple-element.39), channel_id=1, source_target_pairs={{12,0},{16,4},{20,8},{24,12},{28,16},{0,20},{4,24},{8,28},{13,1},{... | collective-permute-start | bytes 56 | tf_op jit(solution)/shard_map/ppermute | solution.py:14
  38.7 4.4 %collective-permute-start.7 = (s32[4]{0:T(128)S(1)}, s32[4]{0:T(128)S(1)}, u32[]{:S(2)}, u32[]{:S(2)}) collective-permute-start(s32[4]{0:T(128)S(1)} %get-tuple-element.38), channel_id=1, source_target_pairs={{16,0},{20,4},{24,8},{28,12},{0,16},{4,20},{8,24},{12,28},{17,1},{... | collective-permute-start | bytes 56 | tf_op jit(solution)/shard_map/ppermute | solution.py:14
  44.0 7.1 %collective-permute-start.8 = (bf16[4,320]{1,0:T(4,128)(2,1)S(1)}, bf16[4,320]{1,0:T(4,128)(2,1)S(1)}, u32[]{:S(2)}, u32[]{:S(2)}) collective-permute-start(bf16[4,320]{1,0:T(4,128)(2,1)S(1)} %get-tuple-element.21), channel_id=1, source_target_pairs={{4,0},{8,4},{12,8},{16,12},{20,16},{24,20},{28,24},{0,28},{5,1},{9... | collective-permute-start | bytes 7688 | tf_op jit(solution)/shard_map/ppermute | solution.py:14
  46.0 6.1 %collective-permute-start.9 = (bf16[4,320]{1,0:T(4,128)(2,1)S(1)}, bf16[4,320]{1,0:T(4,128)(2,1)S(1)}, u32[]{:S(2)}, u32[]{:S(2)}) collective-permute-start(bf16[4,320]{1,0:T(4,128)(2,1)S(1)} %get-tuple-element.20), channel_id=1, source_target_pairs={{8,0},{12,4},{16,8},{20,12},{24,16},{28,20},{0,24},{4,28},{9,1},{1... | collective-permute-start | bytes 7688 | tf_op jit(solution)/shard_map/ppermute | solution.py:14
  47.6 6.4 %collective-permute-start.10 = (bf16[4,320]{1,0:T(4,128)(2,1)S(1)}, bf16[4,320]{1,0:T(4,128)(2,1)S(1)}, u32[]{:S(2)}, u32[]{:S(2)}) collective-permute-start(bf16[4,320]{1,0:T(4,128)(2,1)S(1)} %get-tuple-element.19), channel_id=1, source_target_pairs={{12,0},{16,4},{20,8},{24,12},{28,16},{0,20},{4,24},{8,28},{13,1},{... | collective-permute-start | bytes 7688 | tf_op jit(solution)/shard_map/ppermute | solution.py:14
  48.0 7.9 %collective-permute-start.11 = (bf16[4,320]{1,0:T(4,128)(2,1)S(1)}, bf16[4,320]{1,0:T(4,128)(2,1)S(1)}, u32[]{:S(2)}, u32[]{:S(2)}) collective-permute-start(bf16[4,320]{1,0:T(4,128)(2,1)S(1)} %get-tuple-element.18), channel_id=1, source_target_pairs={{16,0},{20,4},{24,8},{28,12},{0,16},{4,20},{8,24},{12,28},{17,1},{... | collective-permute-start | bytes 7688 | tf_op jit(solution)/shard_map/ppermute | solution.py:14
  50.2 6.3 %collective-permute-start.12 = (bf16[4,320]{1,0:T(4,128)(2,1)S(1)}, bf16[4,320]{1,0:T(4,128)(2,1)S(1)}, u32[]{:S(2)}, u32[]{:S(2)}) collective-permute-start(bf16[4,320]{1,0:T(4,128)(2,1)S(1)} %get-tuple-element.17), channel_id=1, source_target_pairs={{28,0},{0,4},{4,8},{8,12},{12,16},{16,20},{20,24},{24,28},{29,1},{... | collective-permute-start | bytes 7688 | tf_op jit(solution)/shard_map/ppermute | solution.py:14
  51.0 5.5 %collective-permute-start.13 = (bf16[4,320]{1,0:T(4,128)(2,1)S(1)}, bf16[4,320]{1,0:T(4,128)(2,1)S(1)}, u32[]{:S(2)}, u32[]{:S(2)}) collective-permute-start(bf16[4,320]{1,0:T(4,128)(2,1)S(1)} %get-tuple-element.16), channel_id=1, source_target_pairs={{24,0},{28,4},{0,8},{4,12},{8,16},{12,20},{16,24},{20,28},{25,1},{... | collective-permute-start | bytes 7688 | tf_op jit(solution)/shard_map/ppermute | solution.py:14
  52.1 5.4 %collective-permute-start.14 = (bf16[4,320]{1,0:T(4,128)(2,1)S(1)}, bf16[4,320]{1,0:T(4,128)(2,1)S(1)}, u32[]{:S(2)}, u32[]{:S(2)}) collective-permute-start(bf16[4,320]{1,0:T(4,128)(2,1)S(1)} %get-tuple-element.15), channel_id=1, source_target_pairs={{20,0},{24,4},{28,8},{0,12},{4,16},{8,20},{12,24},{16,28},{21,1},{... | collective-permute-start | bytes 7688 | tf_op jit(solution)/shard_map/ppermute | solution.py:14
  54.0 4.6 %collective-permute-start.15 = (bf16[4,320]{1,0:T(4,128)(2,1)S(1)}, bf16[4,320]{1,0:T(4,128)(2,1)S(1)}, u32[]{:S(2)}, u32[]{:S(2)}) collective-permute-start(bf16[4,320]{1,0:T(4,128)(2,1)S(1)} %get-tuple-element.14), channel_id=1, source_target_pairs={{16,0},{20,4},{24,8},{28,12},{0,16},{4,20},{8,24},{12,28},{17,1},{... | collective-permute-start | bytes 7688 | tf_op jit(solution)/shard_map/ppermute | solution.py:14
  60.9 11.7 %collective-permute-start.16 = (f32[4,80]{1,0:T(4,128)S(1)}, f32[4,80]{1,0:T(4,128)S(1)}, u32[]{:S(2)}, u32[]{:S(2)}) collective-permute-start(f32[4,80]{1,0:T(4,128)S(1)} %get-tuple-element.37), channel_id=1, source_target_pairs={{28,0},{0,4},{4,8},{8,12},{12,16},{16,20},{20,24},{24,28},{29,1},{... | collective-permute-start | bytes 3848 | tf_op jit(solution)/shard_map/ppermute | solution.py:14
  64.1 9.5 %collective-permute-start.17 = (f32[4,80]{1,0:T(4,128)S(1)}, f32[4,80]{1,0:T(4,128)S(1)}, u32[]{:S(2)}, u32[]{:S(2)}) collective-permute-start(f32[4,80]{1,0:T(4,128)S(1)} %get-tuple-element.36), channel_id=1, source_target_pairs={{24,0},{28,4},{0,8},{4,12},{8,16},{12,20},{16,24},{20,28},{25,1},{... | collective-permute-start | bytes 3848 | tf_op jit(solution)/shard_map/ppermute | solution.py:14
  65.4 8.6 %collective-permute-start.18 = (f32[4,80]{1,0:T(4,128)S(1)}, f32[4,80]{1,0:T(4,128)S(1)}, u32[]{:S(2)}, u32[]{:S(2)}) collective-permute-start(f32[4,80]{1,0:T(4,128)S(1)} %get-tuple-element.35), channel_id=1, source_target_pairs={{20,0},{24,4},{28,8},{0,12},{4,16},{8,20},{12,24},{16,28},{21,1},{... | collective-permute-start | bytes 3848 | tf_op jit(solution)/shard_map/ppermute | solution.py:14
  67.0 9.0 %collective-permute-start.19 = (f32[4,80]{1,0:T(4,128)S(1)}, f32[4,80]{1,0:T(4,128)S(1)}, u32[]{:S(2)}, u32[]{:S(2)}) collective-permute-start(f32[4,80]{1,0:T(4,128)S(1)} %get-tuple-element.34), channel_id=1, source_target_pairs={{16,0},{20,4},{24,8},{28,12},{0,16},{4,20},{8,24},{12,28},{17,1},{... | collective-permute-start | bytes 3848 | tf_op jit(solution)/shard_map/ppermute | solution.py:14
  70.0 6.0 %collective-permute-start.20 = (f32[4,80]{1,0:T(4,128)S(1)}, f32[4,80]{1,0:T(4,128)S(1)}, u32[]{:S(2)}, u32[]{:S(2)}) collective-permute-start(f32[4,80]{1,0:T(4,128)S(1)} %get-tuple-element.33), channel_id=1, source_target_pairs={{4,0},{8,4},{12,8},{16,12},{20,16},{24,20},{28,24},{0,28},{5,1},{9... | collective-permute-start | bytes 3848 | tf_op jit(solution)/shard_map/ppermute | solution.py:14
  72.6 3.6 %collective-permute-start.21 = (f32[4,80]{1,0:T(4,128)S(1)}, f32[4,80]{1,0:T(4,128)S(1)}, u32[]{:S(2)}, u32[]{:S(2)}) collective-permute-start(f32[4,80]{1,0:T(4,128)S(1)} %get-tuple-element.32), channel_id=1, source_target_pairs={{8,0},{12,4},{16,8},{20,12},{24,16},{28,20},{0,24},{4,28},{9,1},{1... | collective-permute-start | bytes 3848 | tf_op jit(solution)/shard_map/ppermute | solution.py:14
  73.6 4.5 %collective-permute-start.22 = (f32[4,80]{1,0:T(4,128)S(1)}, f32[4,80]{1,0:T(4,128)S(1)}, u32[]{:S(2)}, u32[]{:S(2)}) collective-permute-start(f32[4,80]{1,0:T(4,128)S(1)} %get-tuple-element.31), channel_id=1, source_target_pairs={{12,0},{16,4},{20,8},{24,12},{28,16},{0,20},{4,24},{8,28},{13,1},{... | collective-permute-start | bytes 3848 | tf_op jit(solution)/shard_map/ppermute | solution.py:14
  74.0 4.5 %collective-permute-start.23 = (f32[4,80]{1,0:T(4,128)S(1)}, f32[4,80]{1,0:T(4,128)S(1)}, u32[]{:S(2)}, u32[]{:S(2)}) collective-permute-start(f32[4,80]{1,0:T(4,128)S(1)} %get-tuple-element.30), channel_id=1, source_target_pairs={{16,0},{20,4},{24,8},{28,12},{0,16},{4,20},{8,24},{12,28},{17,1},{... | collective-permute-start | bytes 3848 | tf_op jit(solution)/shard_map/ppermute | solution.py:14
  91.4 9.1 %collective-permute-start.24 = (bf16[4,320]{1,0:T(4,128)(2,1)S(1)}, bf16[4,320]{1,0:T(4,128)(2,1)S(1)}, u32[]{:S(2)}, u32[]{:S(2)}) collective-permute-start(bf16[4,320]{1,0:T(4,128)(2,1)S(1)} %get-tuple-element.13), channel_id=1, source_target_pairs={{4,0},{8,4},{12,8},{16,12},{20,16},{24,20},{28,24},{0,28},{5,1},{9... | collective-permute-start | bytes 7688 | tf_op jit(solution)/shard_map/ppermute | solution.py:14
  94.5 45.9 %copy-start.3 = (f32[8,80]{1,0:T(8,128)S(1)}, f32[8,80]{1,0:T(8,128)}, u32[]{:S(2)}) copy-start(f32[8,80]{1,0:T(8,128)} %param.17) | copy-start | bytes 7684
  95.4 6.1 %collective-permute-start.25 = (bf16[4,320]{1,0:T(4,128)(2,1)S(1)}, bf16[4,320]{1,0:T(4,128)(2,1)S(1)}, u32[]{:S(2)}, u32[]{:S(2)}) collective-permute-start(bf16[4,320]{1,0:T(4,128)(2,1)S(1)} %get-tuple-element.12), channel_id=1, source_target_pairs={{8,0},{12,4},{16,8},{20,12},{24,16},{28,20},{0,24},{4,28},{9,1},{1... | collective-permute-start | bytes 7688 | tf_op jit(solution)/shard_map/ppermute | solution.py:14
  98.0 5.3 %collective-permute-start.26 = (bf16[4,320]{1,0:T(4,128)(2,1)S(1)}, bf16[4,320]{1,0:T(4,128)(2,1)S(1)}, u32[]{:S(2)}, u32[]{:S(2)}) collective-permute-start(bf16[4,320]{1,0:T(4,128)(2,1)S(1)} %get-tuple-element.11), channel_id=1, source_target_pairs={{12,0},{16,4},{20,8},{24,12},{28,16},{0,20},{4,24},{8,28},{13,1},{... | collective-permute-start | bytes 7688 | tf_op jit(solution)/shard_map/ppermute | solution.py:14
  98.0 8.0 %collective-permute-start.27 = (bf16[4,320]{1,0:T(4,128)(2,1)S(1)}, bf16[4,320]{1,0:T(4,128)(2,1)S(1)}, u32[]{:S(2)}, u32[]{:S(2)}) collective-permute-start(bf16[4,320]{1,0:T(4,128)(2,1)S(1)} %get-tuple-element.10), channel_id=1, source_target_pairs={{16,0},{20,4},{24,8},{28,12},{0,16},{4,20},{8,24},{12,28},{17,1},{... | collective-permute-start | bytes 7688 | tf_op jit(solution)/shard_map/ppermute | solution.py:14
  100.6 6.3 %collective-permute-start.28 = (bf16[4,320]{1,0:T(4,128)(2,1)S(1)}, bf16[4,320]{1,0:T(4,128)(2,1)S(1)}, u32[]{:S(2)}, u32[]{:S(2)}) collective-permute-start(bf16[4,320]{1,0:T(4,128)(2,1)S(1)} %get-tuple-element.9), channel_id=1, source_target_pairs={{28,0},{0,4},{4,8},{8,12},{12,16},{16,20},{20,24},{24,28},{29,1},{... | collective-permute-start | bytes 7688 | tf_op jit(solution)/shard_map/ppermute | solution.py:14
  100.6 6.3 %collective-permute-start.29 = (bf16[4,320]{1,0:T(4,128)(2,1)S(1)}, bf16[4,320]{1,0:T(4,128)(2,1)S(1)}, u32[]{:S(2)}, u32[]{:S(2)}) collective-permute-start(bf16[4,320]{1,0:T(4,128)(2,1)S(1)} %get-tuple-element.8), channel_id=1, source_target_pairs={{24,0},{28,4},{0,8},{4,12},{8,16},{12,20},{16,24},{20,28},{25,1},{... | collective-permute-start | bytes 7688 | tf_op jit(solution)/shard_map/ppermute | solution.py:14
  101.5 6.0 %collective-permute-start.30 = (bf16[4,320]{1,0:T(4,128)(2,1)S(1)}, bf16[4,320]{1,0:T(4,128)(2,1)S(1)}, u32[]{:S(2)}, u32[]{:S(2)}) collective-permute-start(bf16[4,320]{1,0:T(4,128)(2,1)S(1)} %get-tuple-element.7), channel_id=1, source_target_pairs={{20,0},{24,4},{28,8},{0,12},{4,16},{8,20},{12,24},{16,28},{21,1},{... | collective-permute-start | bytes 7688 | tf_op jit(solution)/shard_map/ppermute | solution.py:14
  103.3 4.6 %collective-permute-start.31 = (bf16[4,320]{1,0:T(4,128)(2,1)S(1)}, bf16[4,320]{1,0:T(4,128)(2,1)S(1)}, u32[]{:S(2)}, u32[]{:S(2)}) collective-permute-start(bf16[4,320]{1,0:T(4,128)(2,1)S(1)} %get-tuple-element.6), channel_id=1, source_target_pairs={{16,0},{20,4},{24,8},{28,12},{0,16},{4,20},{8,24},{12,28},{17,1},{... | collective-permute-start | bytes 7688 | tf_op jit(solution)/shard_map/ppermute | solution.py:14
  116.0 11.5 %collective-permute-start.32 = (f32[4,80]{1,0:T(4,128)S(1)}, f32[4,80]{1,0:T(4,128)S(1)}, u32[]{:S(2)}, u32[]{:S(2)}) collective-permute-start(f32[4,80]{1,0:T(4,128)S(1)} %get-tuple-element.29), channel_id=1, source_target_pairs={{28,0},{0,4},{4,8},{8,12},{12,16},{16,20},{20,24},{24,28},{29,1},{... | collective-permute-start | bytes 3848 | tf_op jit(solution)/shard_map/ppermute | solution.py:14
  119.8 9.2 %collective-permute-start.33 = (f32[4,80]{1,0:T(4,128)S(1)}, f32[4,80]{1,0:T(4,128)S(1)}, u32[]{:S(2)}, u32[]{:S(2)}) collective-permute-start(f32[4,80]{1,0:T(4,128)S(1)} %get-tuple-element.28), channel_id=1, source_target_pairs={{24,0},{28,4},{0,8},{4,12},{8,16},{12,20},{16,24},{20,28},{25,1},{... | collective-permute-start | bytes 3848 | tf_op jit(solution)/shard_map/ppermute | solution.py:14
  121.4 8.3 %collective-permute-start.34 = (f32[4,80]{1,0:T(4,128)S(1)}, f32[4,80]{1,0:T(4,128)S(1)}, u32[]{:S(2)}, u32[]{:S(2)}) collective-permute-start(f32[4,80]{1,0:T(4,128)S(1)} %get-tuple-element.27), channel_id=1, source_target_pairs={{20,0},{24,4},{28,8},{0,12},{4,16},{8,20},{12,24},{16,28},{21,1},{... | collective-permute-start | bytes 3848 | tf_op jit(solution)/shard_map/ppermute | solution.py:14
  123.8 7.3 %collective-permute-start.35 = (f32[4,80]{1,0:T(4,128)S(1)}, f32[4,80]{1,0:T(4,128)S(1)}, u32[]{:S(2)}, u32[]{:S(2)}) collective-permute-start(f32[4,80]{1,0:T(4,128)S(1)} %get-tuple-element.26), channel_id=1, source_target_pairs={{16,0},{20,4},{24,8},{28,12},{0,16},{4,20},{8,24},{12,28},{17,1},{... | collective-permute-start | bytes 3848 | tf_op jit(solution)/shard_map/ppermute | solution.py:14
  125.2 5.9 %collective-permute-start.36 = (f32[4,80]{1,0:T(4,128)S(1)}, f32[4,80]{1,0:T(4,128)S(1)}, u32[]{:S(2)}, u32[]{:S(2)}) collective-permute-start(f32[4,80]{1,0:T(4,128)S(1)} %get-tuple-element.25), channel_id=1, source_target_pairs={{4,0},{8,4},{12,8},{16,12},{20,16},{24,20},{28,24},{0,28},{5,1},{9... | collective-permute-start | bytes 3848 | tf_op jit(solution)/shard_map/ppermute | solution.py:14
  127.6 3.6 %collective-permute-start.37 = (f32[4,80]{1,0:T(4,128)S(1)}, f32[4,80]{1,0:T(4,128)S(1)}, u32[]{:S(2)}, u32[]{:S(2)}) collective-permute-start(f32[4,80]{1,0:T(4,128)S(1)} %get-tuple-element.24), channel_id=1, source_target_pairs={{8,0},{12,4},{16,8},{20,12},{24,16},{28,20},{0,24},{4,28},{9,1},{1... | collective-permute-start | bytes 3848 | tf_op jit(solution)/shard_map/ppermute | solution.py:14
  129.1 4.5 %collective-permute-start.38 = (f32[4,80]{1,0:T(4,128)S(1)}, f32[4,80]{1,0:T(4,128)S(1)}, u32[]{:S(2)}, u32[]{:S(2)}) collective-permute-start(f32[4,80]{1,0:T(4,128)S(1)} %get-tuple-element.23), channel_id=1, source_target_pairs={{12,0},{16,4},{20,8},{24,12},{28,16},{0,20},{4,24},{8,28},{13,1},{... | collective-permute-start | bytes 3848 | tf_op jit(solution)/shard_map/ppermute | solution.py:14
  129.6 4.5 %collective-permute-start.39 = (f32[4,80]{1,0:T(4,128)S(1)}, f32[4,80]{1,0:T(4,128)S(1)}, u32[]{:S(2)}, u32[]{:S(2)}) collective-permute-start(f32[4,80]{1,0:T(4,128)S(1)} %get-tuple-element.22), channel_id=1, source_target_pairs={{16,0},{20,4},{24,8},{28,12},{0,16},{4,20},{8,24},{12,28},{17,1},{... | collective-permute-start | bytes 3848 | tf_op jit(solution)/shard_map/ppermute | solution.py:14
Sparse Core Ops, SparseCore 0:
  19.8 21.4 reduce-scatter.6
  95.5 18.9 reduce-scatter.8
where the time goes:
time: 155 us
  starting transfers between devices  63 us (41%)
  blocking collectives  33.3 us (21%)
  waiting for transfers between devices  19.1 us (12%)
  between operations  14.4 us (9%)
  local copies, waits for them, and re-layouts  11.5 us (7%)
  other arithmetic  9.07 us (6%)
  matrix products  4.2 us (3%)
    ppermute x40, starting transfers between devices, from_behind(): return lax.ppermute(block, axis, route)  62.9 us
    all_gather x3, blocking collectives, full_rows(): return lax.all_gather(values, 'blk', axis=1, tiled=True)  16.4 us
    ppermute x40, waiting for transfers between devices, from_behind(): return lax.ppermute(block, axis, route)  13.2 us
    all_gather x2, blocking collectives, local(): lax.all_gather((row_terms * mask_rows).astype(jnp.bfloat16), 'blk', axis=...  10.3 us
    psum x1, blocking collectives, local(): indicator = lax.psum(weights, 'blk')  6.6 us
    unnamed x4, waiting for transfers between devices  5.92 us
  transfers between devices with their start and end apart: 42, of which 16 were waited for; matrix products, arithmetic and copies ran while one was open for 7% of the time, Pallas kernels for 0%

commit v1 on v0

v1 whole, which is shorter than its diff:
```python
import functools

import jax
import jax.numpy as jnp
from jax import lax
from jax.experimental import pallas as pl
from jax.experimental.pallas import tpu as pltpu
from jax.sharding import PartitionSpec as P

MODES = 64
SWEEPS = 2
NEIGH = 8
LANES = 128
MESH = pl.DeviceIdType.MESH
NT = (((1,), (1,)), ((), ()))


def slots_of(parts):
    half = NEIGH // 2
    offsets = [0] + list(range(1, half + 1)) + [-k for k in range(1, half + 1)]
    unique, side_slot = [], []
    for offset in offsets:
        wrapped = offset % parts
        if wrapped not in unique:
            unique.append(wrapped)
        side_slot.append(unique.index(wrapped))
    return unique, side_slot


def kernel(
    parts, blocks,
    degree, face_elem, face_side, face_peer, coupling_hbm, inv_diag, inv_off_hbm, source, residual,
    adjoint_out, indicator_out,
    coupling, inv_off, src_buf, state_buf, sent_buf, back_buf, coup_buf, weight_buf,
    load_sem, src_send, src_recv, state_send, state_recv, back_send, back_recv, coup_send, coup_recv,
    weight_send, weight_recv,
):
    unique, side_slot = slots_of(parts)
    slots = len(unique)
    elements, quarter = source.shape
    faces, _, width = coupling.shape
    dom = lax.axis_index("dom")
    blk = lax.axis_index("blk")

    load_inv = pltpu.make_async_copy(inv_off_hbm, inv_off, load_sem.at[0])
    load_coup = pltpu.make_async_copy(coupling_hbm, coupling, load_sem.at[1])
    load_inv.start()
    load_coup.start()

    def siblings():
        return [lax.rem(blk + step, blocks) for step in range(1, blocks)]

    def peers(sign):
        found = []
        for slot in range(slots - 1, 0, -1):
            there = lax.rem(dom + (sign * unique[slot]) % parts, parts)
            found += [(slot, there, k) for k in range(blocks)]
        return found + [(0, dom, k) for k in siblings()]

    barrier = pltpu.get_barrier_semaphore()
    everyone = peers(1)
    for _, there, k in everyone:
        pl.semaphore_signal(barrier, inc=1, device_id=(there, k), device_id_type=MESH)
    pl.semaphore_wait(barrier, len(everyone))

    def send(src, dst, send_sem, recv_sem, there, k):
        pltpu.make_async_remote_copy(
            src_ref=src, dst_ref=dst, send_sem=send_sem, recv_sem=recv_sem,
            device_id=(there, k), device_id_type=MESH,
        ).start()

    def finish(buf, count, sem):
        part = buf.at[pl.ds(0, count)]
        pltpu.make_async_copy(part, part, sem).wait()

    def to_siblings(buf, send_sem, recv_sem):
        for k in siblings():
            send(buf.at[blk], buf.at[blk], send_sem, recv_sem, dom, k)

    def joined(buf, first):
        return jnp.concatenate([buf[first + k][:, :quarter] for k in range(blocks)], axis=1)

    row = lax.broadcasted_iota(jnp.int32, (elements, quarter), 0)
    mode = (lax.broadcasted_iota(jnp.int32, (elements, quarter), 1) + blk * quarter) % MODES
    limit = jnp.zeros((elements, quarter), jnp.int32)
    for e in range(elements):
        step = degree[e] + 1
        limit = jnp.where(row == e, step * step * step * MODES // 64, limit)
    mask = (mode < limit).astype(jnp.float32)

    src_half = (source[...] * mask).astype(jnp.bfloat16).astype(jnp.float32)
    src_buf[blk, :, :quarter] = src_half
    to_siblings(src_buf, src_send, src_recv)

    owner = [face_elem[f] for f in range(faces)]
    target = []
    for f in range(faces):
        side = face_side[f]
        slot = side
        for s, wanted in enumerate(side_slot):
            if wanted != s:
                slot = jnp.where(side == s, wanted, slot)
        target.append(slot * elements + face_peer[f])
    pick_row = lax.broadcasted_iota(jnp.int32, (elements, slots * elements), 0)
    pick_col = lax.broadcasted_iota(jnp.int32, (elements, slots * elements), 1)
    pick = jnp.concatenate(
        [
            jnp.where((pick_row == owner[f]) & (pick_col == target[f]), 1.0, 0.0)
            for f in range(faces)
        ],
        axis=0,
    ).astype(jnp.bfloat16)
    target_row = lax.broadcasted_iota(jnp.int32, (slots * elements, quarter), 0)
    full_row = lax.broadcasted_iota(jnp.int32, (elements, width), 0)

    def invert(own, full):
        total = inv_diag[...] * own
        for e in range(elements):
            left = jnp.where(full_row == e, full, 0.0).astype(jnp.bfloat16)
            total += lax.dot_general(left, inv_off[e], NT, preferred_element_type=jnp.float32)
        return total

    finish(src_buf, blocks - 1, src_recv)
    load_inv.wait()
    base = invert(src_half, joined(src_buf, 0)) * mask
    load_coup.wait()

    adjoint = base
    for sweep in range(SWEEPS):
        state, sent, back, coup = (
            buf.at[sweep] for buf in (state_buf, sent_buf, back_buf, coup_buf)
        )
        own_state = adjoint.astype(jnp.bfloat16).astype(jnp.float32)
        state[blk, :, :quarter] = own_state
        for slot, there, k in peers(-1):
            send(state.at[blk], state.at[slot * blocks + blk],
                 state_send.at[sweep], state_recv.at[sweep], there, k)

        turned = jnp.zeros((slots * elements, width), jnp.float32)
        for f in range(faces):
            line = jnp.sum(jnp.where(row == owner[f], own_state, 0.0), axis=0, keepdims=True)
            left = jnp.where(target_row == target[f], line, 0.0).astype(jnp.bfloat16)
            turned += jnp.dot(left, coupling[f], preferred_element_type=jnp.float32)
        for slot in range(slots):
            for k in range(blocks):
                sent[slot * blocks + k, :, :quarter] = turned[
                    slot * elements:(slot + 1) * elements, k * quarter:(k + 1) * quarter
                ]
        for slot, there, k in peers(1):
            send(sent.at[slot * blocks + k], back.at[slot * blocks + blk],
                 back_send.at[sweep], back_recv.at[sweep], there, k)
        coupled = sent[blk][:, :quarter]

        finish(state, slots * blocks - 1, state_recv.at[sweep])
        every = jnp.concatenate([joined(state, slot * blocks) for slot in range(slots)], axis=0)
        picked = jnp.dot(pick, every.astype(jnp.bfloat16), preferred_element_type=jnp.float32)
        for f in range(faces):
            left = picked[f * elements:(f + 1) * elements].astype(jnp.bfloat16)
            coupled += lax.dot_general(left, coupling[f], NT, preferred_element_type=jnp.float32)

        finish(back, slots * blocks - 1, back_recv.at[sweep])
        for step in range(1, blocks):
            coupled += back[lax.rem(blk + step, blocks)][:, :quarter]
        for place in range(blocks, slots * blocks):
            coupled += back[place][:, :quarter]
        half = (coupled * mask).astype(jnp.bfloat16).astype(jnp.float32)
        coup[blk, :, :quarter] = half
        to_siblings(coup, coup_send.at[sweep], coup_recv.at[sweep])
        finish(coup, blocks - 1, coup_recv.at[sweep])
        adjoint = (base - invert(half, joined(coup, 0))) * mask

    adjoint_out[...] = adjoint
    weights = jnp.sum(adjoint * residual[...] * mask, axis=1, keepdims=True)
    lane = lax.broadcasted_iota(jnp.int32, (elements, LANES), 1)
    sub = lax.broadcasted_iota(jnp.int32, (elements, LANES), 0)
    weight_buf[blk] = jnp.where(lane == sub, weights, 0.0)
    to_siblings(weight_buf, weight_send, weight_recv)
    finish(weight_buf, blocks - 1, weight_recv)
    total = weight_buf[0]
    for k in range(1, blocks):
        total += weight_buf[k]
    indicator_out[...] = jnp.sum(total, axis=0, keepdims=True)[:, :elements]

    finish(src_buf, blocks - 1, src_send)
    finish(weight_buf, blocks - 1, weight_send)
    for sweep in range(SWEEPS):
        finish(state_buf.at[sweep], slots * blocks - 1, state_send.at[sweep])
        finish(back_buf.at[sweep], slots * blocks - 1, back_send.at[sweep])
        finish(coup_buf.at[sweep], blocks - 1, coup_send.at[sweep])


def local(degree, face_elem, face_side, face_peer, coupling, inv_diag, inv_off, source, residual):
    elements, quarter = source.shape
    parts, blocks = lax.axis_size("dom"), lax.axis_size("blk")
    places = len(slots_of(parts)[0]) * blocks
    smem = pl.BlockSpec(memory_space=pltpu.SMEM)
    vmem = pl.BlockSpec(memory_space=pltpu.VMEM)
    hbm = pl.BlockSpec(memory_space=pl.ANY)
    tile = (elements, LANES)
    dma = pltpu.SemaphoreType.DMA
    adjoint, indicator = pl.pallas_call(
        functools.partial(kernel, parts, blocks),
        out_shape=(
            jax.ShapeDtypeStruct((elements, quarter), jnp.float32),
            jax.ShapeDtypeStruct((1, elements), jnp.float32),
        ),
        in_specs=[smem, smem, smem, smem, hbm, vmem, hbm, vmem, vmem],
        out_specs=(vmem, vmem),
        scratch_shapes=[
            pltpu.VMEM(coupling.shape, coupling.dtype),
            pltpu.VMEM(inv_off.shape, inv_off.dtype),
            pltpu.VMEM((blocks,) + tile, jnp.float32),
            pltpu.VMEM((SWEEPS, places) + tile, jnp.float32),
            pltpu.VMEM((SWEEPS, places) + tile, jnp.float32),
            pltpu.VMEM((SWEEPS, places) + tile, jnp.float32),
            pltpu.VMEM((SWEEPS, blocks) + tile, jnp.float32),
            pltpu.VMEM((blocks,) + tile, jnp.float32),
            dma((2,)), dma, dma,
            dma((SWEEPS,)), dma((SWEEPS,)), dma((SWEEPS,)), dma((SWEEPS,)),
            dma((SWEEPS,)), dma((SWEEPS,)),
            dma, dma,
        ],
        compiler_params=pltpu.CompilerParams(
            collective_id=0, has_side_effects=True, vmem_limit_bytes=40 * 2**20
        ),
    )(degree, face_elem, face_side, face_peer, coupling, inv_diag, inv_off, source, residual)
    return adjoint, indicator.reshape(elements)


def solution(mesh):
    in_specs = (
        P("dom"),
        P("dom"),
        P("dom"),
        P("dom"),
        P("dom", "blk", None),
        P("dom", "blk"),
        P("dom", "blk", None),
        P("dom", "blk"),
        P("dom", "blk"),
    )
    out_specs = (P("dom", "blk"), P("dom"))
    return jax.shard_map(local, mesh=mesh, in_specs=in_specs, out_specs=out_specs, check_vma=False)
```

time: 155 us -> 46.1 us (0.30)
  starting transfers between devices: 63 us -> 0 us
  Pallas kernels: 0 us -> 36.8 us
  blocking collectives: 33.3 us -> 0 us
  waiting for transfers between devices: 19.1 us -> 0 us
  between operations: 14.4 us -> 0.66 us
  other arithmetic: 9.07 us -> 0 us
  matrix products: 4.2 us -> 0 us
  local copies, waits for them, and re-layouts: 11.5 us -> 8.35 us
    ppermute x40 -> x0, starting transfers between devices: 62.9 us -> none  [from_behind(): return lax.ppermute(block, axis, route)]
    pallas_call x0 -> x1, Pallas kernels: none -> 36.8 us  [local(): pl.pallas_call(functools.partial(kernel, parts, blocks), out_shape=(jax.S...]
    all_gather x5 -> x0, blocking collectives: 26.7 us -> none  [the longest x3 16.4 us: full_rows(): return lax.all_gather(values, 'blk', axis=1, tiled=True)]
    ppermute x40 -> x0, waiting for transfers between devices: 13.2 us -> none  [from_behind(): return lax.ppermute(block, axis, route)]
    psum x1 -> x0, blocking collectives: 6.6 us -> none  [local(): indicator = lax.psum(weights, 'blk')]
    unnamed x4 -> x0, waiting for transfers between devices: 5.92 us -> none
    unnamed x54 -> x20, local copies, waits for them, and re-layouts: 2.43 us -> 8.35 us
    gather x8 -> x0, local copies, waits for them, and re-layouts: 4.99 us -> none  [the longest x2 1.27 us: local(): state_full[face_peer]]
  transfers between devices with their start and end apart: 42 -> 0, of which waited for: 16 -> 0; matrix products, arithmetic and copies ran while one was open for 7% -> 0% of each run, Pallas kernels for 0% -> 0%
where the time goes in v1:
time: 46.1 us; the launch traced here: 45.8 us
  Pallas kernels  36.8 us (80%)
  local copies, waits for them, and re-layouts  8.35 us (18%)
  between operations  0.66 us (1%)
    pallas_call x1, Pallas kernels, local(): pl.pallas_call(functools.partial(kernel, parts, blocks), out_shape=(jax.S...  36.8 us
    unnamed x20, local copies, waits for them, and re-layouts  8.35 us

profile of v1, /device:TPU:0, one launch (start us, length us, event | category | flops | bytes accessed | tf_op | source)
XLA Modules:
  0.0 45.8 jit_solution(16051835877507918902)
XLA Ops:
  0.6 0.0 copy-start
  0.6 1.5 %copy-done = bf16[32,80,320]{2,1,0:T(8,128)(2,1)S(1)} copy-done((bf16[32,80,320]{2,1,0:T(8,128)(2,1)S(1)}, bf16[32,80,320]{2,1,0:T(8,128)(2,1)}, u32[]{:S(2)}) %copy-start) | copy-done | bytes 1638424
  2.2 0.0 copy-start.1
  2.2 1.0 %copy-done.1 = bf16[8,80,320]{2,1,0:T(8,128)(2,1)S(1)} copy-done((bf16[8,80,320]{2,1,0:T(8,128)(2,1)S(1)}, bf16[8,80,320]{2,1,0:T(8,128)(2,1)}, u32[]{:S(2)}) %copy-start.1) | copy-done | bytes 409624
  3.2 0.0 copy-start.2
  3.2 0.7 %copy-done.2 = f32[8,80]{1,0:T(8,128)S(1)} copy-done((f32[8,80]{1,0:T(8,128)S(1)}, f32[8,80]{1,0:T(8,128)}, u32[]{:S(2)}) %copy-start.2) | copy-done | bytes 2584
  3.9 0.0 copy-start.3
  3.9 0.7 %copy-done.3 = f32[8,80]{1,0:T(8,128)S(1)} copy-done((f32[8,80]{1,0:T(8,128)S(1)}, f32[8,80]{1,0:T(8,128)}, u32[]{:S(2)}) %copy-start.3) | copy-done | bytes 2584
  4.6 0.0 copy-start.4
  4.6 0.7 %copy-done.4 = f32[8,80]{1,0:T(8,128)S(1)} copy-done((f32[8,80]{1,0:T(8,128)S(1)}, f32[8,80]{1,0:T(8,128)}, u32[]{:S(2)}) %copy-start.4) | copy-done | bytes 2584
  5.3 0.0 copy-start.5
  5.3 0.7 %copy-done.5 = s32[8]{0:T(128)S(1)} copy-done((s32[8]{0:T(128)S(1)}, s32[8]{0:T(128)}, u32[]{:S(2)}) %copy-start.5) | copy-done | bytes 56
  5.9 0.0 copy-start.6
  5.9 0.7 %copy-done.6 = s32[32]{0:T(128)S(1)} copy-done((s32[32]{0:T(128)S(1)}, s32[32]{0:T(128)}, u32[]{:S(2)}) %copy-start.6) | copy-done | bytes 152
  6.6 0.0 copy-start.7
  6.6 0.7 %copy-done.7 = s32[32]{0:T(128)S(1)} copy-done((s32[32]{0:T(128)S(1)}, s32[32]{0:T(128)}, u32[]{:S(2)}) %copy-start.7) | copy-done | bytes 152
  7.2 0.0 copy-start.8
  7.2 0.7 %copy-done.8 = s32[32]{0:T(128)S(1)} copy-done((s32[32]{0:T(128)S(1)}, s32[32]{0:T(128)}, u32[]{:S(2)}) %copy-start.8) | copy-done | bytes 152
  7.9 36.8 %shard_map.104 = (f32[8,80]{1,0:T(8,128)S(1)}, f32[1,8]{1,0:T(1,128)S(1)}) custom-call(s32[8]{0:T(128)S(1)} %copy-done.5, s32[32]{0:T(128)S(1)} %copy-done.6, s32[32]{0:T(128)S(1)} %copy-done.7, s32[32]{0:T(128)S(1)} %copy-done.8, bf16[32,80,320]{2,1,0:T(8,128)(2,1)S(1)} %copy-done, f32[8,80]{1,0:T(8,128)S(1)} %copy-done.2, ...), custom_call_target="tpu_custom_call" | custom-call | tf_op jit(solution)/shard_map/pallas_call | solution.py:201
  44.7 0.6 %copy.13 = f32[8,80]{1,0:T(8,128)} copy(f32[8,80]{1,0:T(8,128)S(1)} %get-tuple-element.8) | data formatting | bytes 5120
  45.3 0.5 %copy.14 = f32[8]{0:T(128)} copy(f32[8]{0:T(128)S(1)} %bitcast.1) | data formatting | bytes 64
Async XLA Ops:
  0.6 1.5 %copy-start = (bf16[32,80,320]{2,1,0:T(8,128)(2,1)S(1)}, bf16[32,80,320]{2,1,0:T(8,128)(2,1)}, u32[]{:S(2)}) copy-start(bf16[32,80,320]{2,1,0:T(8,128)(2,1)} %coupling_hbm.1) | copy-start | bytes 4915204
  2.2 1.0 %copy-start.1 = (bf16[8,80,320]{2,1,0:T(8,128)(2,1)S(1)}, bf16[8,80,320]{2,1,0:T(8,128)(2,1)}, u32[]{:S(2)}) copy-start(bf16[8,80,320]{2,1,0:T(8,128)(2,1)} %inv_off_hbm.1) | copy-start | bytes 1228804
  3.2 0.7 %copy-start.2 = (f32[8,80]{1,0:T(8,128)S(1)}, f32[8,80]{1,0:T(8,128)}, u32[]{:S(2)}) copy-start(f32[8,80]{1,0:T(8,128)} %inv_diag.1) | copy-start | bytes 7684
  3.9 0.7 %copy-start.3 = (f32[8,80]{1,0:T(8,128)S(1)}, f32[8,80]{1,0:T(8,128)}, u32[]{:S(2)}) copy-start(f32[8,80]{1,0:T(8,128)} %source.1) | copy-start | bytes 7684
  4.6 0.7 %copy-start.4 = (f32[8,80]{1,0:T(8,128)S(1)}, f32[8,80]{1,0:T(8,128)}, u32[]{:S(2)}) copy-start(f32[8,80]{1,0:T(8,128)} %residual.1) | copy-start | bytes 7684
  5.3 0.7 %copy-start.5 = (s32[8]{0:T(128)S(1)}, s32[8]{0:T(128)}, u32[]{:S(2)}) copy-start(s32[8]{0:T(128)} %degree.1) | copy-start | bytes 100
  5.9 0.7 %copy-start.6 = (s32[32]{0:T(128)S(1)}, s32[32]{0:T(128)}, u32[]{:S(2)}) copy-start(s32[32]{0:T(128)} %face_elem.1) | copy-start | bytes 388
  6.6 0.7 %copy-start.7 = (s32[32]{0:T(128)S(1)}, s32[32]{0:T(128)}, u32[]{:S(2)}) copy-start(s32[32]{0:T(128)} %face_side.1) | copy-start | bytes 388
  7.2 0.7 %copy-start.8 = (s32[32]{0:T(128)S(1)}, s32[32]{0:T(128)}, u32[]{:S(2)}) copy-start(s32[32]{0:T(128)} %face_peer.1) | copy-start | bytes 388

commit v2 on v1

v2 whole, which is shorter than its diff:
```python
import functools

import jax
import jax.numpy as jnp
from jax import lax
from jax.experimental import pallas as pl
from jax.experimental.pallas import tpu as pltpu
from jax.sharding import PartitionSpec as P

MODES = 64
SWEEPS = 2
NEIGH = 8
LANES = 128
MESH = pl.DeviceIdType.MESH
NT = (((1,), (1,)), ((), ()))


def slots_of(parts):
    half = NEIGH // 2
    offsets = [0] + list(range(1, half + 1)) + [-k for k in range(1, half + 1)]
    unique, side_slot = [], []
    for offset in offsets:
        wrapped = offset % parts
        if wrapped not in unique:
            unique.append(wrapped)
        side_slot.append(unique.index(wrapped))
    return unique, side_slot


def kernel(
    parts, blocks,
    degree_hbm, elem_hbm, side_hbm, peer_hbm, coupling_hbm, diag_hbm, inv_off_hbm, source_hbm,
    residual_hbm,
    adjoint_out, indicator_out,
    degree, face_elem, face_side, face_peer, coupling, inv_diag, inv_off, source, residual,
    src_buf, state_buf, wide_buf, sent_buf, part_buf, out_buf, back_buf, coup_buf, dual_buf,
    load_sem, src_sem, dual_sem, state_sem, wide_sem, part_sem, back_sem, coup_sem,
):
    unique, side_slot = slots_of(parts)
    slots = len(unique)
    elements, quarter = source.shape
    faces, _, width = coupling.shape
    table = slots * elements
    dom = lax.axis_index("dom")
    blk = lax.axis_index("blk")

    loads = [
        pltpu.make_async_copy(src, dst, load_sem.at[place])
        for place, (src, dst) in enumerate([
            (degree_hbm, degree), (source_hbm, source), (elem_hbm, face_elem),
            (side_hbm, face_side), (peer_hbm, face_peer), (diag_hbm, inv_diag),
            (residual_hbm, residual), (inv_off_hbm, inv_off), (coupling_hbm, coupling),
        ])
    ]
    for load in loads:
        load.start()

    siblings = [lax.rem(blk + step, blocks) for step in range(1, blocks)]

    def away(slot, sign):
        return lax.rem(dom + (sign * unique[slot]) % parts, parts)

    barrier = pltpu.get_barrier_semaphore()
    for slot in range(1, slots):
        pl.semaphore_signal(
            barrier, inc=1, device_id=(away(slot, 1), blk), device_id_type=MESH
        )
    for k in siblings:
        pl.semaphore_signal(barrier, inc=1, device_id=(dom, k), device_id_type=MESH)

    def send(src, dst, sems, there, k):
        pltpu.make_async_remote_copy(
            src_ref=src, dst_ref=dst, send_sem=sems.at[0], recv_sem=sems.at[1],
            device_id=(there, k), device_id_type=MESH,
        ).start()

    def finish(buf, count, sem):
        part = buf.at[pl.ds(0, count)]
        pltpu.make_async_copy(part, part, sem).wait()

    def to_siblings(buf, sems):
        for k in siblings:
            send(buf.at[blk], buf.at[blk], sems, dom, k)

    def joined(buf, rows):
        return jnp.concatenate(
            [buf[k][:rows, :quarter].astype(jnp.float32) for k in range(blocks)], axis=1
        )

    row = lax.broadcasted_iota(jnp.int32, (elements, quarter), 0)
    mode = (lax.broadcasted_iota(jnp.int32, (elements, quarter), 1) + blk * quarter) % MODES
    limit = jnp.zeros((elements, quarter), jnp.int32)
    loads[0].wait()
    for e in range(elements):
        step = degree[e] + 1
        limit = jnp.where(row == e, step * step * step * MODES // 64, limit)
    mask = (mode < limit).astype(jnp.float32)
    loads[1].wait()
    src_half = (source[...] * mask).astype(jnp.bfloat16).astype(jnp.float32)
    src_buf[blk, :, :quarter] = src_half

    pl.semaphore_wait(barrier, slots - 1 + blocks - 1)
    to_siblings(src_buf, src_sem)

    for load in loads[2:7]:
        load.wait()
    owner = [face_elem[f] for f in range(faces)]
    target = []
    for f in range(faces):
        side = face_side[f]
        slot = side
        for s, wanted in enumerate(side_slot):
            if wanted != s:
                slot = jnp.where(side == s, wanted, slot)
        target.append(slot * elements + face_peer[f])

    weight = residual[...] * mask
    high = weight.astype(jnp.bfloat16).astype(jnp.float32)
    low = weight - high
    row16 = lax.broadcasted_iota(jnp.int32, (2 * elements, quarter), 0)
    both = jnp.concatenate([high, low], axis=0)
    loads[7].wait()
    dual = jnp.zeros((2 * elements, width), jnp.float32)
    for e in range(elements):
        left = jnp.where((row16 == e) | (row16 == e + elements), both, 0.0).astype(jnp.bfloat16)
        dual += jnp.dot(left, inv_off[e], preferred_element_type=jnp.float32)
    dual = dual[:elements] + dual[elements:]
    own_dual = weight * inv_diag[...]
    own_cols = lax.broadcasted_iota(jnp.int32, (elements, width), 1)
    spread = jnp.concatenate([own_dual] * blocks, axis=1)
    mine = (own_cols >= blk * quarter) & (own_cols < (blk + 1) * quarter)
    dual_buf[blk, :, :width] = dual + jnp.where(mine, spread, 0.0)

    pick_row = lax.broadcasted_iota(jnp.int32, (elements, table), 0)
    pick_col = lax.broadcasted_iota(jnp.int32, (elements, table), 1)
    pick = jnp.concatenate(
        [
            jnp.where((pick_row == owner[f]) & (pick_col == target[f]), 1.0, 0.0)
            for f in range(faces)
        ],
        axis=0,
    ).astype(jnp.bfloat16)
    group = max(1, 256 // quarter)
    starts = list(range(0, faces, group))
    spread_row = lax.broadcasted_iota(jnp.int32, (table, group * elements), 0)
    spread_col = lax.broadcasted_iota(jnp.int32, (table, group * elements), 1)
    place_of = []
    for first in starts:
        hot = jnp.zeros((table, group * elements), jnp.float32)
        for f in range(first, min(first + group, faces)):
            col = (f - first) * elements + owner[f]
            hot = jnp.where((spread_row == target[f]) & (spread_col == col), 1.0, hot)
        place_of.append(hot)
    place_of = jnp.concatenate(place_of, axis=0).astype(jnp.bfloat16)
    group_col = lax.broadcasted_iota(jnp.int32, (elements, group * quarter), 1)
    wide_lane = lax.broadcasted_iota(jnp.int32, (quarter, faces * elements), 1)
    fold_row = lax.broadcasted_iota(jnp.int32, (elements, faces * elements), 0)
    fold_col = lax.broadcasted_iota(jnp.int32, (elements, faces * elements), 1)
    fold = jnp.where(fold_col % elements == fold_row, 1.0, 0.0)
    full_row = lax.broadcasted_iota(jnp.int32, (elements, width), 0)

    def invert(own, full):
        total = inv_diag[...] * own
        for e in range(elements):
            left = jnp.where(full_row == e, full, 0.0).astype(jnp.bfloat16)
            total += lax.dot_general(left, inv_off[e], NT, preferred_element_type=jnp.float32)
        return total

    finish(src_buf, blocks - 1, src_sem.at[1])
    base = invert(src_half, joined(src_buf, elements)) * mask
    loads[8].wait()

    adjoint = base
    for sweep in range(SWEEPS):
        state, wide, sent, part, out, back, coup = (
            buf.at[sweep]
            for buf in (state_buf, wide_buf, sent_buf, part_buf, out_buf, back_buf, coup_buf)
        )
        state_sems, wide_sems, part_sems, back_sems, coup_sems = (
            sems.at[sweep] for sems in (state_sem, wide_sem, part_sem, back_sem, coup_sem)
        )
        own_state = adjoint.astype(jnp.bfloat16).astype(jnp.float32)
        state[0, :, :quarter] = own_state
        for slot in range(1, slots):
            send(state.at[0], state.at[slot], state_sems, away(slot, -1), blk)

        repeated = jnp.concatenate([own_state] * group, axis=1)
        stacked = jnp.concatenate(
            [
                jnp.where(
                    (group_col >= g * quarter) & (group_col < (g + 1) * quarter), repeated, 0.0
                )
                for g in range(group)
            ],
            axis=0,
        ).astype(jnp.bfloat16)
        lefts = jnp.dot(place_of, stacked, preferred_element_type=jnp.float32)
        turned = jnp.zeros((table, width), jnp.float32)
        for index, first in enumerate(starts):
            last = min(first + group, faces)
            depth = (last - first) * quarter
            left = lefts[index * table:(index + 1) * table, :depth].astype(jnp.bfloat16)
            turned += jnp.dot(
                left, coupling[first:last].reshape(depth, width),
                preferred_element_type=jnp.float32,
            )
        for k in range(blocks):
            sent[k, :, :, :quarter] = turned[:, k * quarter:(k + 1) * quarter].reshape(
                slots, elements, quarter
            )
        for k in siblings:
            send(sent.at[k], part.at[blk], part_sems, dom, k)

        if sweep == 0:
            dual_buf[blk, :, width:] = jnp.broadcast_to(
                jnp.sum(weight * base, axis=1, keepdims=True),
                (elements, dual_buf.shape[2] - width),
            )
            to_siblings(dual_buf, dual_sem)

        finish(state, slots - 1, state_sems.at[1])
        column = state[...].reshape(table, LANES)
        if wide.shape[1] > table:
            column = jnp.concatenate(
                [column, jnp.zeros((wide.shape[1] - table, LANES), jnp.float32)], axis=0
            )
        wide[blk] = column.astype(jnp.bfloat16)
        to_siblings(wide, wide_sems)

        finish(part, blocks - 1, part_sems.at[1])
        total = sent[blk]
        for k in siblings:
            total += part[k]
        out[...] = total
        for slot in range(1, slots):
            send(out.at[slot], back.at[slot], back_sems, away(slot, 1), blk)
        coupled = total[0][:, :quarter]

        finish(wide, blocks - 1, wide_sems.at[1])
        every = joined(wide, table).astype(jnp.bfloat16)
        picked = jnp.dot(pick, every, preferred_element_type=jnp.float32).astype(jnp.bfloat16)
        product = lax.dot_general(
            coupling[...].reshape(faces * quarter, width), picked, NT,
            preferred_element_type=jnp.float32,
        )
        held = jnp.zeros((quarter, faces * elements), jnp.float32)
        for f in range(faces):
            chosen = (wide_lane >= f * elements) & (wide_lane < (f + 1) * elements)
            held = jnp.where(chosen, product[f * quarter:(f + 1) * quarter], held)
        coupled += lax.dot_general(
            fold, held, NT, precision=lax.Precision.HIGHEST, preferred_element_type=jnp.float32
        )

        finish(back, slots - 1, back_sems.at[1])
        for slot in range(1, slots):
            coupled += back[slot][:, :quarter]
        half = (coupled * mask).astype(jnp.bfloat16).astype(jnp.float32)
        coup[blk, :, :quarter] = half
        to_siblings(coup, coup_sems)
        finish(coup, blocks - 1, coup_sems.at[1])
        full = joined(coup, elements)
        adjoint = (base - invert(half, full)) * mask

    adjoint_out[...] = adjoint
    finish(dual_buf, blocks - 1, dual_sem.at[1])
    dual = dual_buf[0]
    for k in range(1, blocks):
        dual += dual_buf[k]
    weights = dual[:, width:width + 1] - jnp.sum(dual[:, :width] * full, axis=1, keepdims=True)
    lane = lax.broadcasted_iota(jnp.int32, (elements, elements), 1)
    sub = lax.broadcasted_iota(jnp.int32, (elements, elements), 0)
    indicator_out[...] = jnp.sum(jnp.where(lane == sub, weights, 0.0), axis=0, keepdims=True)

    finish(src_buf, blocks - 1, src_sem.at[0])
    finish(dual_buf, blocks - 1, dual_sem.at[0])
    for sweep in range(SWEEPS):
        finish(state_buf.at[sweep], slots - 1, state_sem.at[sweep, 0])
        finish(wide_buf.at[sweep], blocks - 1, wide_sem.at[sweep, 0])
        finish(part_buf.at[sweep], blocks - 1, part_sem.at[sweep, 0])
        finish(back_buf.at[sweep], slots - 1, back_sem.at[sweep, 0])
        finish(coup_buf.at[sweep], blocks - 1, coup_sem.at[sweep, 0])


def local(degree, face_elem, face_side, face_peer, coupling, inv_diag, inv_off, source, residual):
    elements, quarter = source.shape
    parts, blocks = lax.axis_size("dom"), lax.axis_size("blk")
    width = coupling.shape[2]
    slots = len(slots_of(parts)[0])
    vmem = pl.BlockSpec(memory_space=pltpu.VMEM)
    hbm = pl.BlockSpec(memory_space=pl.ANY)
    tile = (elements, LANES)
    rows = -(-slots * elements // 16) * 16
    dual_width = (width // LANES + 1) * LANES
    dma = pltpu.SemaphoreType.DMA
    args = (degree, face_elem, face_side, face_peer, coupling, inv_diag, inv_off, source, residual)
    adjoint, indicator = pl.pallas_call(
        functools.partial(kernel, parts, blocks),
        out_shape=(
            jax.ShapeDtypeStruct((elements, quarter), jnp.float32),
            jax.ShapeDtypeStruct((1, elements), jnp.float32),
        ),
        in_specs=[hbm] * len(args),
        out_specs=(vmem, vmem),
        scratch_shapes=[pltpu.SMEM(arg.shape, arg.dtype) for arg in args[:4]]
        + [pltpu.VMEM(arg.shape, arg.dtype) for arg in args[4:]]
        + [
            pltpu.VMEM((blocks,) + tile, jnp.float32),
            pltpu.VMEM((SWEEPS, slots) + tile, jnp.float32),
            pltpu.VMEM((SWEEPS, blocks, rows, LANES), jnp.bfloat16),
            pltpu.VMEM((SWEEPS, blocks, slots) + tile, jnp.float32),
            pltpu.VMEM((SWEEPS, blocks, slots) + tile, jnp.float32),
            pltpu.VMEM((SWEEPS, slots) + tile, jnp.float32),
            pltpu.VMEM((SWEEPS, slots) + tile, jnp.float32),
            pltpu.VMEM((SWEEPS, blocks) + tile, jnp.float32),
            pltpu.VMEM((blocks, elements, dual_width), jnp.float32),
            dma((len(args),)), dma((2,)), dma((2,)),
        ]
        + [dma((SWEEPS, 2))] * 5,
        compiler_params=pltpu.CompilerParams(
            collective_id=0, has_side_effects=True, vmem_limit_bytes=60 * 2**20
        ),
    )(*args)
    return adjoint, indicator.reshape(elements)


def solution(mesh):
    in_specs = (
        P("dom"),
        P("dom"),
        P("dom"),
        P("dom"),
        P("dom", "blk", None),
        P("dom", "blk"),
        P("dom", "blk", None),
        P("dom", "blk"),
        P("dom", "blk"),
    )
    out_specs = (P("dom", "blk"), P("dom"))
    return jax.shard_map(local, mesh=mesh, in_specs=in_specs, out_specs=out_specs, check_vma=False)
```

time: 46.1 us -> 37.5 us (0.81)
  local copies, waits for them, and re-layouts: 8.35 us -> 2.4 us
  Pallas kernels: 36.8 us -> 34.3 us
    unnamed x20 -> x2, local copies, waits for them, and re-layouts: 8.35 us -> 2.4 us
    pallas_call x1, Pallas kernels: 36.8 us -> 34.3 us  [local(): pl.pallas_call(functools.partial(kernel, parts, blocks), out_shape=(jax.S...]
where the time goes in v2:
time: 37.5 us; the launch traced here: 37.4 us
  Pallas kernels  34.3 us (91%)
  local copies, waits for them, and re-layouts  2.4 us (6%)
  between operations  0.64 us (2%)
    pallas_call x1, Pallas kernels, local(): pl.pallas_call(functools.partial(kernel, parts, blocks), out_shape=(jax.S...  34.3 us
    unnamed x2, local copies, waits for them, and re-layouts  2.4 us

profile of v2, /device:TPU:0, one launch (start us, length us, event | category | flops | bytes accessed | tf_op | source)
XLA Modules:
  0.0 37.4 jit_solution(4450550414986842971)
XLA Ops:
  0.6 34.3 %shard_map.104 = (f32[8,80]{1,0:T(8,128)}, f32[1,8]{1,0:T(1,128)}) custom-call(s32[8]{0:T(128)} %degree_hbm.1, s32[32]{0:T(128)} %elem_hbm.1, s32[32]{0:T(128)} %side_hbm.1, s32[32]{0:T(128)} %peer_hbm.1, bf16[32,80,320]{2,1,0:T(8,128)(2,1)} %coupling_hbm.1, f32[8,80]{1,0:T(8,128)} %diag_hbm.1, bf16[8,80,320]{2,1,0:T(8,128)(2,1)} %inv_off_hbm.1, ...), custom_call_target="tpu_custom_call" | custom-call | tf_op jit(solution)/shard_map/pallas_call | solution.py:296
  35.0 1.3 %copy.13 = f32[8,80]{1,0:T(8,128)} copy(f32[8,80]{1,0:T(8,128)} %get-tuple-element.8) | data formatting | bytes 5120
  36.2 1.1 %copy.14 = f32[8]{0:T(128)} copy(f32[8]{0:T(128)} %bitcast.1) | data formatting | bytes 64

commit v3 on v2

--- a/solution.py
+++ b/solution.py
@@ -31,10 +31,10 @@
     parts, blocks,
     degree_hbm, elem_hbm, side_hbm, peer_hbm, coupling_hbm, diag_hbm, inv_off_hbm, source_hbm,
     residual_hbm,
-    adjoint_out, indicator_out,
+    result_out,
     degree, face_elem, face_side, face_peer, coupling, inv_diag, inv_off, source, residual,
-    src_buf, state_buf, wide_buf, sent_buf, part_buf, out_buf, back_buf, coup_buf, dual_buf,
-    load_sem, src_sem, dual_sem, state_sem, wide_sem, part_sem, back_sem, coup_sem,
+    src_buf, state_buf, wide_buf, sent_buf, back_buf, coup_buf, dual_buf,
+    load_sem, src_sem, dual_sem, state_sem, wide_sem, back_sem, coup_sem,
 ):
     unique, side_slot = slots_of(parts)
     slots = len(unique)
@@ -89,12 +89,29 @@
 
     row = lax.broadcasted_iota(jnp.int32, (elements, quarter), 0)
     mode = (lax.broadcasted_iota(jnp.int32, (elements, quarter), 1) + blk * quarter) % MODES
+    full_row = lax.broadcasted_iota(jnp.int32, (elements, width), 0)
+    full_col = lax.broadcasted_iota(jnp.int32, (elements, width), 1)
+    mine = (full_col >= blk * quarter) & (full_col < (blk + 1) * quarter)
+
+    def in_place(values):
+        return jnp.where(mine, jnp.concatenate([values] * blocks, axis=1), 0.0)
+
+    def own_part(values):
+        found = values[:, :quarter]
+        for k in range(1, blocks):
+            found = jnp.where(blk == k, values[:, k * quarter:(k + 1) * quarter], found)
+        return found
+
     limit = jnp.zeros((elements, quarter), jnp.int32)
+    full_limit = jnp.zeros((elements, width), jnp.int32)
     loads[0].wait()
     for e in range(elements):
         step = degree[e] + 1
-        limit = jnp.where(row == e, step * step * step * MODES // 64, limit)
+        count = step * step * step * MODES // 64
+        limit = jnp.where(row == e, count, limit)
+        full_limit = jnp.where(full_row == e, count, full_limit)
     mask = (mode < limit).astype(jnp.float32)
+    full_mask = (full_col % MODES < full_limit).astype(jnp.float32)
     loads[1].wait()
     src_half = (source[...] * mask).astype(jnp.bfloat16).astype(jnp.float32)
     src_buf[blk, :, :quarter] = src_half
@@ -125,11 +142,7 @@
         left = jnp.where((row16 == e) | (row16 == e + elements), both, 0.0).astype(jnp.bfloat16)
         dual += jnp.dot(left, inv_off[e], preferred_element_type=jnp.float32)
     dual = dual[:elements] + dual[elements:]
-    own_dual = weight * inv_diag[...]
-    own_cols = lax.broadcasted_iota(jnp.int32, (elements, width), 1)
-    spread = jnp.concatenate([own_dual] * blocks, axis=1)
-    mine = (own_cols >= blk * quarter) & (own_cols < (blk + 1) * quarter)
-    dual_buf[blk, :, :width] = dual + jnp.where(mine, spread, 0.0)
+    dual_buf[blk, :, :width] = dual + in_place(weight * inv_diag[...])
 
     pick_row = lax.broadcasted_iota(jnp.int32, (elements, table), 0)
     pick_col = lax.broadcasted_iota(jnp.int32, (elements, table), 1)
@@ -157,7 +170,6 @@
     fold_row = lax.broadcasted_iota(jnp.int32, (elements, faces * elements), 0)
     fold_col = lax.broadcasted_iota(jnp.int32, (elements, faces * elements), 1)
     fold = jnp.where(fold_col % elements == fold_row, 1.0, 0.0)
-    full_row = lax.broadcasted_iota(jnp.int32, (elements, width), 0)
 
     def invert(own, full):
         total = inv_diag[...] * own
@@ -168,16 +180,18 @@
 
     finish(src_buf, blocks - 1, src_sem.at[1])
     base = invert(src_half, joined(src_buf, elements)) * mask
+    dual_buf[blk, :, width:] = jnp.broadcast_to(
+        jnp.sum(weight * base, axis=1, keepdims=True), (elements, dual_buf.shape[2] - width)
+    )
     loads[8].wait()
 
-    adjoint = base
-    for sweep in range(SWEEPS):
-        state, wide, sent, part, out, back, coup = (
-            buf.at[sweep]
-            for buf in (state_buf, wide_buf, sent_buf, part_buf, out_buf, back_buf, coup_buf)
-        )
-        state_sems, wide_sems, part_sems, back_sems, coup_sems = (
-            sems.at[sweep] for sems in (state_sem, wide_sem, part_sem, back_sem, coup_sem)
+    def one_sweep(sweep, carry):
+        adjoint, _ = carry
+        state, wide, sent, back, coup = (
+            buf.at[sweep] for buf in (state_buf, wide_buf, sent_buf, back_buf, coup_buf)
+        )
+        state_sems, wide_sems, back_sems, coup_sems = (
+            sems.at[sweep] for sems in (state_sem, wide_sem, back_sem, coup_sem)
         )
         own_state = adjoint.astype(jnp.bfloat16).astype(jnp.float32)
         state[0, :, :quarter] = own_state
@@ -204,19 +218,9 @@
                 left, coupling[first:last].reshape(depth, width),
                 preferred_element_type=jnp.float32,
             )
-        for k in range(blocks):
-            sent[k, :, :, :quarter] = turned[:, k * quarter:(k + 1) * quarter].reshape(
-                slots, elements, quarter
-            )
-        for k in siblings:
-            send(sent.at[k], part.at[blk], part_sems, dom, k)
-
-        if sweep == 0:
-            dual_buf[blk, :, width:] = jnp.broadcast_to(
-                jnp.sum(weight * base, axis=1, keepdims=True),
-                (elements, dual_buf.shape[2] - width),
-            )
-            to_siblings(dual_buf, dual_sem)
+        sent[:, :, :width] = turned.reshape(slots, elements, width)
+        for slot in range(1, slots):
+            send(sent.at[slot], back.at[slot], back_sems, away(slot, 1), blk)
 
         finish(state, slots - 1, state_sems.at[1])
         column = state[...].reshape(table, LANES)
@@ -227,15 +231,6 @@
         wide[blk] = column.astype(jnp.bfloat16)
         to_siblings(wide, wide_sems)
 
-        finish(part, blocks - 1, part_sems.at[1])
-        total = sent[blk]
-        for k in siblings:
-            total += part[k]
-        out[...] = total
-        for slot in range(1, slots):
-            send(out.at[slot], back.at[slot], back_sems, away(slot, 1), blk)
-        coupled = total[0][:, :quarter]
-
         finish(wide, blocks - 1, wide_sems.at[1])
         every = joined(wide, table).astype(jnp.bfloat16)
         picked = jnp.dot(pick, every, preferred_element_type=jnp.float32).astype(jnp.bfloat16)
@@ -247,36 +242,45 @@
         for f in range(faces):
             chosen = (wide_lane >= f * elements) & (wide_lane < (f + 1) * elements)
             held = jnp.where(chosen, product[f * quarter:(f + 1) * quarter], held)
-        coupled += lax.dot_general(
+        own_terms = lax.dot_general(
             fold, held, NT, precision=lax.Precision.HIGHEST, preferred_element_type=jnp.float32
         )
+        partial = turned[:elements] + in_place(own_terms)
 
         finish(back, slots - 1, back_sems.at[1])
         for slot in range(1, slots):
-            coupled += back[slot][:, :quarter]
-        half = (coupled * mask).astype(jnp.bfloat16).astype(jnp.float32)
-        coup[blk, :, :quarter] = half
+            partial += back[slot][:, :width]
+        coup[blk, :, :width] = partial
         to_siblings(coup, coup_sems)
         finish(coup, blocks - 1, coup_sems.at[1])
-        full = joined(coup, elements)
-        adjoint = (base - invert(half, full)) * mask
-
-    adjoint_out[...] = adjoint
+        coupled = coup[0]
+        for k in range(1, blocks):
+            coupled += coup[k]
+        full = (coupled[:, :width] * full_mask).astype(jnp.bfloat16).astype(jnp.float32)
+        return (base - invert(own_part(full), full)) * mask, full
+
+    to_siblings(dual_buf, dual_sem)
+    adjoint, full = lax.fori_loop(
+        0, SWEEPS, one_sweep, (base, jnp.zeros((elements, width), jnp.float32))
+    )
+
+    result_out[:elements, :quarter] = adjoint
     finish(dual_buf, blocks - 1, dual_sem.at[1])
     dual = dual_buf[0]
     for k in range(1, blocks):
         dual += dual_buf[k]
     weights = dual[:, width:width + 1] - jnp.sum(dual[:, :width] * full, axis=1, keepdims=True)
-    lane = lax.broadcasted_iota(jnp.int32, (elements, elements), 1)
-    sub = lax.broadcasted_iota(jnp.int32, (elements, elements), 0)
-    indicator_out[...] = jnp.sum(jnp.where(lane == sub, weights, 0.0), axis=0, keepdims=True)
+    lane = lax.broadcasted_iota(jnp.int32, (elements, LANES), 1)
+    sub = lax.broadcasted_iota(jnp.int32, (elements, LANES), 0)
+    result_out[elements:elements + 1, :] = jnp.sum(
+        jnp.where(lane == sub, weights, 0.0), axis=0, keepdims=True
+    )
 
     finish(src_buf, blocks - 1, src_sem.at[0])
     finish(dual_buf, blocks - 1, dual_sem.at[0])
     for sweep in range(SWEEPS):
         finish(state_buf.at[sweep], slots - 1, state_sem.at[sweep, 0])
         finish(wide_buf.at[sweep], blocks - 1, wide_sem.at[sweep, 0])
-        finish(part_buf.at[sweep], blocks - 1, part_sem.at[sweep, 0])
         finish(back_buf.at[sweep], slots - 1, back_sem.at[sweep, 0])
         finish(coup_buf.at[sweep], blocks - 1, coup_sem.at[sweep, 0])
 
@@ -291,36 +295,32 @@
     tile = (elements, LANES)
     rows = -(-slots * elements // 16) * 16
     dual_width = (width // LANES + 1) * LANES
+    full_width = -(-width // LANES) * LANES
     dma = pltpu.SemaphoreType.DMA
     args = (degree, face_elem, face_side, face_peer, coupling, inv_diag, inv_off, source, residual)
-    adjoint, indicator = pl.pallas_call(
+    result = pl.pallas_call(
         functools.partial(kernel, parts, blocks),
-        out_shape=(
-            jax.ShapeDtypeStruct((elements, quarter), jnp.float32),
-            jax.ShapeDtypeStruct((1, elements), jnp.float32),
-        ),
+        out_shape=jax.ShapeDtypeStruct((2 * elements, LANES), jnp.float32),
         in_specs=[hbm] * len(args),
-        out_specs=(vmem, vmem),
+        out_specs=vmem,
         scratch_shapes=[pltpu.SMEM(arg.shape, arg.dtype) for arg in args[:4]]
         + [pltpu.VMEM(arg.shape, arg.dtype) for arg in args[4:]]
         + [
             pltpu.VMEM((blocks,) + tile, jnp.float32),
             pltpu.VMEM((SWEEPS, slots) + tile, jnp.float32),
             pltpu.VMEM((SWEEPS, blocks, rows, LANES), jnp.bfloat16),
-            pltpu.VMEM((SWEEPS, blocks, slots) + tile, jnp.float32),
-            pltpu.VMEM((SWEEPS, blocks, slots) + tile, jnp.float32),
-            pltpu.VMEM((SWEEPS, slots) + tile, jnp.float32),
-            pltpu.VMEM((SWEEPS, slots) + tile, jnp.float32),
-            pltpu.VMEM((SWEEPS, blocks) + tile, jnp.float32),
+            pltpu.VMEM((SWEEPS, slots, elements, full_width), jnp.float32),
+            pltpu.VMEM((SWEEPS, slots, elements, full_width), jnp.float32),
+            pltpu.VMEM((SWEEPS, blocks, elements, full_width), jnp.float32),
             pltpu.VMEM((blocks, elements, dual_width), jnp.float32),
             dma((len(args),)), dma((2,)), dma((2,)),
         ]
-        + [dma((SWEEPS, 2))] * 5,
+        + [dma((SWEEPS, 2))] * 4,
         compiler_params=pltpu.CompilerParams(
             collective_id=0, has_side_effects=True, vmem_limit_bytes=60 * 2**20
         ),
     )(*args)
-    return adjoint, indicator.reshape(elements)
+    return result[:elements, :quarter], result[elements, :elements]
 
 
 def solution(mesh):

time: 37.5 us -> 37.3 us (level)
    unnamed x2 -> x0, local copies, waits for them, and re-layouts: 2.4 us -> none
    slice x0 -> x1, local copies, waits for them, and re-layouts: none -> 1.27 us  [local(): return (result[:elements, :quarter], result[elements, :elements])]
    squeeze x0 -> x1, local copies, waits for them, and re-layouts: none -> 1.19 us  [local(): return (result[:elements, :quarter], result[elements, :elements])]
where the time goes in v3:
time: 37.3 us; the launch traced here: 37.1 us
  Pallas kernels  34 us (91%)
  local copies, waits for them, and re-layouts  2.47 us (7%)
  between operations  0.64 us (2%)
    pallas_call x1, Pallas kernels, local(): pl.pallas_call(functools.partial(kernel, parts, blocks), out_shape=jax.Sh...  34 us
    slice x1, local copies, waits for them, and re-layouts, local(): return (result[:elements, :quarter], result[elements, :elements])  1.27 us
    squeeze x1, local copies, waits for them, and re-layouts, local(): return (result[:elements, :quarter], result[elements, :elements])  1.19 us

profile of v3, /device:TPU:0, one launch (start us, length us, event | category | flops | bytes accessed | tf_op | source)
XLA Modules:
  0.0 37.1 jit_solution(18217975690195691002)
XLA Ops:
  0.6 34.0 %shard_map.104 = f32[16,128]{1,0:T(8,128)} custom-call(s32[8]{0:T(128)} %degree_hbm.1, s32[32]{0:T(128)} %elem_hbm.1, s32[32]{0:T(128)} %side_hbm.1, s32[32]{0:T(128)} %peer_hbm.1, bf16[32,80,320]{2,1,0:T(8,128)(2,1)} %coupling_hbm.1, f32[8,80]{1,0:T(8,128)} %diag_hbm.1, bf16[8,80,320]{2,1,0:T(8,128)(2,1)} %inv_off_hbm.1, f32[8,80]{1,0:T(8,128)} %source_hbm.1, ...), custom_call_target="tpu_custom_call" | custom-call | tf_op jit(solution)/shard_map/pallas_call | solution.py:301
  34.6 1.2 %slice_bitcast_fusion = f32[8]{0:T(128)} fusion(f32[16,128]{1,0:T(8,128)} %shard_map.104), kind=kLoop, calls=%fused_computation | loop fusion | bytes 64 | tf_op jit(solution)/shard_map/squeeze | solution.py:323
  35.8 1.3 %slice.6 = f32[8,80]{1,0:T(8,128)} slice(f32[16,128]{1,0:T(8,128)} %shard_map.104), slice={[0:8], [0:80]} | slice | bytes 5120 | tf_op jit(solution)/shard_map/slice | solution.py:323

commit v4 on v3

--- a/solution.py
+++ b/solution.py
@@ -1,4 +1,5 @@
 import functools
+import math
 
 import jax
 import jax.numpy as jnp
@@ -33,8 +34,8 @@
     residual_hbm,
     result_out,
     degree, face_elem, face_side, face_peer, coupling, inv_diag, inv_off, source, residual,
-    src_buf, state_buf, wide_buf, sent_buf, back_buf, coup_buf, dual_buf,
-    load_sem, src_sem, dual_sem, state_sem, wide_sem, back_sem, coup_sem,
+    src_buf, state_buf, sent_buf, back_buf, coup_buf, dual_buf,
+    load_sem, src_sem, dual_sem, state_sem, back_sem, coup_sem,
 ):
     unique, side_slot = slots_of(parts)
     slots = len(unique)
@@ -62,9 +63,10 @@
 
     barrier = pltpu.get_barrier_semaphore()
     for slot in range(1, slots):
-        pl.semaphore_signal(
-            barrier, inc=1, device_id=(away(slot, 1), blk), device_id_type=MESH
-        )
+        for k in range(blocks):
+            pl.semaphore_signal(
+                barrier, inc=1, device_id=(away(slot, 1), k), device_id_type=MESH
+            )
     for k in siblings:
         pl.semaphore_signal(barrier, inc=1, device_id=(dom, k), device_id_type=MESH)
 
@@ -116,7 +118,7 @@
     src_half = (source[...] * mask).astype(jnp.bfloat16).astype(jnp.float32)
     src_buf[blk, :, :quarter] = src_half
 
-    pl.semaphore_wait(barrier, slots - 1 + blocks - 1)
+    pl.semaphore_wait(barrier, slots * blocks - 1)
     to_siblings(src_buf, src_sem)
 
     for load in loads[2:7]:
@@ -166,10 +168,11 @@
         place_of.append(hot)
     place_of = jnp.concatenate(place_of, axis=0).astype(jnp.bfloat16)
     group_col = lax.broadcasted_iota(jnp.int32, (elements, group * quarter), 1)
-    wide_lane = lax.broadcasted_iota(jnp.int32, (quarter, faces * elements), 1)
-    fold_row = lax.broadcasted_iota(jnp.int32, (elements, faces * elements), 0)
-    fold_col = lax.broadcasted_iota(jnp.int32, (elements, faces * elements), 1)
-    fold = jnp.where(fold_col % elements == fold_row, 1.0, 0.0)
+    chunk = math.gcd(faces, max(1, LANES // elements))
+    chunk_lane = lax.broadcasted_iota(jnp.int32, (quarter, chunk * elements), 1)
+    fold_row = lax.broadcasted_iota(jnp.int32, (elements, 2 * chunk * elements), 0)
+    fold_col = lax.broadcasted_iota(jnp.int32, (elements, 2 * chunk * elements), 1)
+    fold = jnp.where(fold_col % elements == fold_row, 1.0, 0.0).astype(jnp.bfloat16)
 
     def invert(own, full):
         total = inv_diag[...] * own
@@ -187,16 +190,20 @@
 
     def one_sweep(sweep, carry):
         adjoint, _ = carry
-        state, wide, sent, back, coup = (
-            buf.at[sweep] for buf in (state_buf, wide_buf, sent_buf, back_buf, coup_buf)
+        state, sent, back, coup = (
+            buf.at[sweep] for buf in (state_buf, sent_buf, back_buf, coup_buf)
         )
-        state_sems, wide_sems, back_sems, coup_sems = (
-            sems.at[sweep] for sems in (state_sem, wide_sem, back_sem, coup_sem)
+        state_sems, back_sems, coup_sems = (
+            sems.at[sweep] for sems in (state_sem, back_sem, coup_sem)
         )
         own_state = adjoint.astype(jnp.bfloat16).astype(jnp.float32)
-        state[0, :, :quarter] = own_state
+        state[blk] = jnp.concatenate(
+            [own_state, jnp.zeros((elements, LANES - quarter), jnp.float32)], axis=1
+        ).astype(jnp.bfloat16)
         for slot in range(1, slots):
-            send(state.at[0], state.at[slot], state_sems, away(slot, -1), blk)
+            for k in range(blocks):
+                send(state.at[blk], state.at[slot * blocks + blk], state_sems, away(slot, -1), k)
+        to_siblings(state, state_sems)
 
         repeated = jnp.concatenate([own_state] * group, axis=1)
         stacked = jnp.concatenate(
@@ -222,28 +229,36 @@
         for slot in range(1, slots):
             send(sent.at[slot], back.at[slot], back_sems, away(slot, 1), blk)
 
-        finish(state, slots - 1, state_sems.at[1])
-        column = state[...].reshape(table, LANES)
-        if wide.shape[1] > table:
-            column = jnp.concatenate(
-                [column, jnp.zeros((wide.shape[1] - table, LANES), jnp.float32)], axis=0
+        finish(state, slots * blocks - 1, state_sems.at[1])
+        every = jnp.concatenate(
+            [
+                jnp.concatenate(
+                    [
+                        state[slot * blocks + k].astype(jnp.float32)[:, :quarter]
+                        for k in range(blocks)
+                    ],
+                    axis=1,
+                )
+                for slot in range(slots)
+            ],
+            axis=0,
+        ).astype(jnp.bfloat16)
+        picked = jnp.dot(pick, every, preferred_element_type=jnp.float32).astype(jnp.bfloat16)
+        held = jnp.zeros((quarter, chunk * elements), jnp.float32)
+        for first in range(0, faces, chunk):
+            product = lax.dot_general(
+                coupling[first:first + chunk].reshape(chunk * quarter, width),
+                picked[first * elements:(first + chunk) * elements],
+                NT,
+                preferred_element_type=jnp.float32,
             )
-        wide[blk] = column.astype(jnp.bfloat16)
-        to_siblings(wide, wide_sems)
-
-        finish(wide, blocks - 1, wide_sems.at[1])
-        every = joined(wide, table).astype(jnp.bfloat16)
-        picked = jnp.dot(pick, every, preferred_element_type=jnp.float32).astype(jnp.bfloat16)
-        product = lax.dot_general(
-            coupling[...].reshape(faces * quarter, width), picked, NT,
-            preferred_element_type=jnp.float32,
-        )
-        held = jnp.zeros((quarter, faces * elements), jnp.float32)
-        for f in range(faces):
-            chosen = (wide_lane >= f * elements) & (wide_lane < (f + 1) * elements)
-            held = jnp.where(chosen, product[f * quarter:(f + 1) * quarter], held)
+            for f in range(chunk):
+                chosen = (chunk_lane >= f * elements) & (chunk_lane < (f + 1) * elements)
+                held += jnp.where(chosen, product[f * quarter:(f + 1) * quarter], 0.0)
+        high = held.astype(jnp.bfloat16)
+        low = (held - high.astype(jnp.float32)).astype(jnp.bfloat16)
         own_terms = lax.dot_general(
-            fold, held, NT, precision=lax.Precision.HIGHEST, preferred_element_type=jnp.float32
+            fold, jnp.concatenate([high, low], axis=1), NT, preferred_element_type=jnp.float32
         )
         partial = turned[:elements] + in_place(own_terms)
 
@@ -279,10 +294,15 @@
     finish(src_buf, blocks - 1, src_sem.at[0])
     finish(dual_buf, blocks - 1, dual_sem.at[0])
     for sweep in range(SWEEPS):
-        finish(state_buf.at[sweep], slots - 1, state_sem.at[sweep, 0])
-        finish(wide_buf.at[sweep], blocks - 1, wide_sem.at[sweep, 0])
+        finish(state_buf.at[sweep], slots * blocks - 1, state_sem.at[sweep, 0])
         finish(back_buf.at[sweep], slots - 1, back_sem.at[sweep, 0])
         finish(coup_buf.at[sweep], blocks - 1, coup_sem.at[sweep, 0])
+
+
+def split_result(result, adjoint, indicator):
+    elements, quarter = adjoint.shape
+    adjoint[...] = result[:elements, :quarter]
+    indicator[...] = result[elements:elements + 1, :elements]
 
 
 def local(degree, face_elem, face_side, face_peer, coupling, inv_diag, inv_off, source, residual):
@@ -293,7 +313,6 @@
     vmem = pl.BlockSpec(memory_space=pltpu.VMEM)
     hbm = pl.BlockSpec(memory_space=pl.ANY)
     tile = (elements, LANES)
-    rows = -(-slots * elements // 16) * 16
     dual_width = (width // LANES + 1) * LANES
     full_width = -(-width // LANES) * LANES
     dma = pltpu.SemaphoreType.DMA
@@ -307,20 +326,28 @@
         + [pltpu.VMEM(arg.shape, arg.dtype) for arg in args[4:]]
         + [
             pltpu.VMEM((blocks,) + tile, jnp.float32),
-            pltpu.VMEM((SWEEPS, slots) + tile, jnp.float32),
-            pltpu.VMEM((SWEEPS, blocks, rows, LANES), jnp.bfloat16),
+            pltpu.VMEM((SWEEPS, slots * blocks) + tile, jnp.bfloat16),
             pltpu.VMEM((SWEEPS, slots, elements, full_width), jnp.float32),
             pltpu.VMEM((SWEEPS, slots, elements, full_width), jnp.float32),
             pltpu.VMEM((SWEEPS, blocks, elements, full_width), jnp.float32),
             pltpu.VMEM((blocks, elements, dual_width), jnp.float32),
             dma((len(args),)), dma((2,)), dma((2,)),
         ]
-        + [dma((SWEEPS, 2))] * 4,
+        + [dma((SWEEPS, 2))] * 3,
         compiler_params=pltpu.CompilerParams(
             collective_id=0, has_side_effects=True, vmem_limit_bytes=60 * 2**20
         ),
     )(*args)
-    return result[:elements, :quarter], result[elements, :elements]
+    adjoint, indicator = pl.pallas_call(
+        split_result,
+        out_shape=(
+            jax.ShapeDtypeStruct((elements, quarter), jnp.float32),
+            jax.ShapeDtypeStruct((1, elements), jnp.float32),
+        ),
+        in_specs=[vmem],
+        out_specs=(vmem, vmem),
+    )(result)
+    return adjoint, indicator.reshape(elements)
 
 
 def solution(mesh):

time: 37.3 us -> 31.6 us (0.85)
  Pallas kernels: 34 us -> 30.8 us
  local copies, waits for them, and re-layouts: 2.47 us -> 0 us
    pallas_call x1, Pallas kernels: 34 us -> 29.5 us  [local(): pl.pallas_call(functools.partial(kernel, parts, blocks), out_shape=jax.Sh...]
    pallas_call x0 -> x1, Pallas kernels: none -> 1.29 us  [local(): pl.pallas_call(split_result, out_shape=(jax.ShapeDtypeStruct((elements, q...]
    slice x1 -> x0, local copies, waits for them, and re-layouts: 1.27 us -> none  [local(): return (result[:elements, :quarter], result[elements, :elements])]
    squeeze x1 -> x0, local copies, waits for them, and re-layouts: 1.19 us -> none  [local(): return (result[:elements, :quarter], result[elements, :elements])]
where the time goes in v4:
time: 31.6 us; the launch traced here: 31.4 us
  Pallas kernels  30.8 us (97%)
  between operations  0.64 us (2%)
    pallas_call x1, Pallas kernels, local(): pl.pallas_call(functools.partial(kernel, parts, blocks), out_shape=jax.Sh...  29.5 us
    pallas_call x1, Pallas kernels, local(): pl.pallas_call(split_result, out_shape=(jax.ShapeDtypeStruct((elements, q...  1.29 us

profile of v4, /device:TPU:0, one launch (start us, length us, event | category | flops | bytes accessed | tf_op | source)
XLA Modules:
  0.0 31.4 jit_solution(3142185144467181401)
XLA Ops:
  0.6 29.5 %shard_map.104.result = f32[16,128]{1,0:T(8,128)} custom-call(s32[8]{0:T(128)} %degree_hbm.1, s32[32]{0:T(128)} %elem_hbm.1, s32[32]{0:T(128)} %side_hbm.1, s32[32]{0:T(128)} %peer_hbm.1, bf16[32,80,320]{2,1,0:T(8,128)(2,1)} %coupling_hbm.1, f32[8,80]{1,0:T(8,128)} %diag_hbm.1, bf16[8,80,320]{2,1,0:T(8,128)(2,1)} %inv_off_hbm.1, f32[8,80]{1,0:T(8,128)} %source_hbm.1, ...), custom_call_target="tpu_custom_call" | custom-call | tf_op jit(solution)/shard_map/pallas_call | solution.py:320
  30.1 1.3 %shard_map.105 = (f32[8,80]{1,0:T(8,128)}, f32[1,8]{1,0:T(1,128)}) custom-call(f32[16,128]{1,0:T(8,128)} %shard_map.104.result), custom_call_target="tpu_custom_call" | custom-call | tf_op jit(solution)/shard_map/pallas_call | solution.py:341

commit v5 on v4

--- a/solution.py
+++ b/solution.py
@@ -118,9 +118,6 @@
     src_half = (source[...] * mask).astype(jnp.bfloat16).astype(jnp.float32)
     src_buf[blk, :, :quarter] = src_half
 
-    pl.semaphore_wait(barrier, slots * blocks - 1)
-    to_siblings(src_buf, src_sem)
-
     for load in loads[2:7]:
         load.wait()
     owner = [face_elem[f] for f in range(faces)]
@@ -132,19 +129,6 @@
             if wanted != s:
                 slot = jnp.where(side == s, wanted, slot)
         target.append(slot * elements + face_peer[f])
-
-    weight = residual[...] * mask
-    high = weight.astype(jnp.bfloat16).astype(jnp.float32)
-    low = weight - high
-    row16 = lax.broadcasted_iota(jnp.int32, (2 * elements, quarter), 0)
-    both = jnp.concatenate([high, low], axis=0)
-    loads[7].wait()
-    dual = jnp.zeros((2 * elements, width), jnp.float32)
-    for e in range(elements):
-        left = jnp.where((row16 == e) | (row16 == e + elements), both, 0.0).astype(jnp.bfloat16)
-        dual += jnp.dot(left, inv_off[e], preferred_element_type=jnp.float32)
-    dual = dual[:elements] + dual[elements:]
-    dual_buf[blk, :, :width] = dual + in_place(weight * inv_diag[...])
 
     pick_row = lax.broadcasted_iota(jnp.int32, (elements, table), 0)
     pick_col = lax.broadcasted_iota(jnp.int32, (elements, table), 1)
@@ -174,6 +158,22 @@
     fold_col = lax.broadcasted_iota(jnp.int32, (elements, 2 * chunk * elements), 1)
     fold = jnp.where(fold_col % elements == fold_row, 1.0, 0.0).astype(jnp.bfloat16)
 
+    pl.semaphore_wait(barrier, slots * blocks - 1)
+    to_siblings(src_buf, src_sem)
+
+    weight = residual[...] * mask
+    high = weight.astype(jnp.bfloat16).astype(jnp.float32)
+    low = weight - high
+    row16 = lax.broadcasted_iota(jnp.int32, (2 * elements, quarter), 0)
+    both = jnp.concatenate([high, low], axis=0)
+    loads[7].wait()
+    dual = jnp.zeros((2 * elements, width), jnp.float32)
+    for e in range(elements):
+        left = jnp.where((row16 == e) | (row16 == e + elements), both, 0.0).astype(jnp.bfloat16)
+        dual += jnp.dot(left, inv_off[e], preferred_element_type=jnp.float32)
+    dual = dual[:elements] + dual[elements:]
+    dual_buf[blk, :, :width] = dual + in_place(weight * inv_diag[...])
+
     def invert(own, full):
         total = inv_diag[...] * own
         for e in range(elements):
@@ -225,7 +225,7 @@
                 left, coupling[first:last].reshape(depth, width),
                 preferred_element_type=jnp.float32,
             )
-        sent[:, :, :width] = turned.reshape(slots, elements, width)
+        sent[:, :, :width] = turned.reshape(slots, elements, width).astype(jnp.bfloat16)
         for slot in range(1, slots):
             send(sent.at[slot], back.at[slot], back_sems, away(slot, 1), blk)
 
@@ -264,7 +264,7 @@
 
         finish(back, slots - 1, back_sems.at[1])
         for slot in range(1, slots):
-            partial += back[slot][:, :width]
+            partial += back[slot].astype(jnp.float32)[:, :width]
         coup[blk, :, :width] = partial
         to_siblings(coup, coup_sems)
         finish(coup, blocks - 1, coup_sems.at[1])
@@ -327,8 +327,8 @@
         + [
             pltpu.VMEM((blocks,) + tile, jnp.float32),
             pltpu.VMEM((SWEEPS, slots * blocks) + tile, jnp.bfloat16),
-            pltpu.VMEM((SWEEPS, slots, elements, full_width), jnp.float32),
-            pltpu.VMEM((SWEEPS, slots, elements, full_width), jnp.float32),
+            pltpu.VMEM((SWEEPS, slots, elements, full_width), jnp.bfloat16),
+            pltpu.VMEM((SWEEPS, slots, elements, full_width), jnp.bfloat16),
             pltpu.VMEM((SWEEPS, blocks, elements, full_width), jnp.float32),
             pltpu.VMEM((blocks, elements, dual_width), jnp.float32),
             dma((len(args),)), dma((2,)), dma((2,)),
@@ -346,6 +346,7 @@
         ),
         in_specs=[vmem],
         out_specs=(vmem, vmem),
+        compiler_params=pltpu.CompilerParams(vmem_limit_bytes=60 * 2**20),
     )(result)
     return adjoint, indicator.reshape(elements)
 

time: 31.6 us -> 30.6 us (0.968)
  Pallas kernels: 30.8 us -> 29.8 us
    pallas_call x1, Pallas kernels: 29.5 us -> 28.5 us  [local(): pl.pallas_call(functools.partial(kernel, parts, blocks), out_shape=jax.Sh...]
where the time goes in v5:
time: 30.6 us; the launch traced here: 30.4 us
  Pallas kernels  29.8 us (97%)
  between operations  0.64 us (2%)
    pallas_call x1, Pallas kernels, local(): pl.pallas_call(functools.partial(kernel, parts, blocks), out_shape=jax.Sh...  28.5 us
    pallas_call x1, Pallas kernels, local(): pl.pallas_call(split_result, out_shape=(jax.ShapeDtypeStruct((elements, q...  1.29 us

profile of v5, /device:TPU:0, one launch (start us, length us, event | category | flops | bytes accessed | tf_op | source)
XLA Modules:
  0.0 30.4 jit_solution(12526046462984783121)
XLA Ops:
  0.6 28.5 %shard_map.104.result = f32[16,128]{1,0:T(8,128)} custom-call(s32[8]{0:T(128)} %degree_hbm.1, s32[32]{0:T(128)} %elem_hbm.1, s32[32]{0:T(128)} %side_hbm.1, s32[32]{0:T(128)} %peer_hbm.1, bf16[32,80,320]{2,1,0:T(8,128)(2,1)} %coupling_hbm.1, f32[8,80]{1,0:T(8,128)} %diag_hbm.1, bf16[8,80,320]{2,1,0:T(8,128)(2,1)} %inv_off_hbm.1, f32[8,80]{1,0:T(8,128)} %source_hbm.1, ...), custom_call_target="tpu_custom_call" | custom-call | tf_op jit(solution)/shard_map/pallas_call | solution.py:320
  29.1 1.3 %shard_map.105 = (f32[8,80]{1,0:T(8,128)}, f32[1,8]{1,0:T(1,128)}) custom-call(f32[16,128]{1,0:T(8,128)} %shard_map.104.result), custom_call_target="tpu_custom_call" | custom-call | tf_op jit(solution)/shard_map/pallas_call | solution.py:341

commit v6 on v5

--- a/solution.py
+++ b/solution.py
@@ -45,6 +45,20 @@
     dom = lax.axis_index("dom")
     blk = lax.axis_index("blk")
 
+    siblings = [lax.rem(blk + step, blocks) for step in range(1, blocks)]
+
+    def away(slot, sign):
+        return lax.rem(dom + (sign * unique[slot]) % parts, parts)
+
+    barrier = pltpu.get_barrier_semaphore()
+    for slot in range(1, slots):
+        for k in range(blocks):
+            pl.semaphore_signal(
+                barrier, inc=1, device_id=(away(slot, 1), k), device_id_type=MESH
+            )
+    for k in siblings:
+        pl.semaphore_signal(barrier, inc=1, device_id=(dom, k), device_id_type=MESH)
+
     loads = [
         pltpu.make_async_copy(src, dst, load_sem.at[place])
         for place, (src, dst) in enumerate([
@@ -55,20 +69,6 @@
     ]
     for load in loads:
         load.start()
-
-    siblings = [lax.rem(blk + step, blocks) for step in range(1, blocks)]
-
-    def away(slot, sign):
-        return lax.rem(dom + (sign * unique[slot]) % parts, parts)
-
-    barrier = pltpu.get_barrier_semaphore()
-    for slot in range(1, slots):
-        for k in range(blocks):
-            pl.semaphore_signal(
-                barrier, inc=1, device_id=(away(slot, 1), k), device_id_type=MESH
-            )
-    for k in siblings:
-        pl.semaphore_signal(barrier, inc=1, device_id=(dom, k), device_id_type=MESH)
 
     def send(src, dst, sems, there, k):
         pltpu.make_async_remote_copy(
@@ -188,8 +188,9 @@
     )
     loads[8].wait()
 
-    def one_sweep(sweep, carry):
-        adjoint, _ = carry
+    to_siblings(dual_buf, dual_sem)
+    adjoint = base
+    for sweep in range(SWEEPS):
         state, sent, back, coup = (
             buf.at[sweep] for buf in (state_buf, sent_buf, back_buf, coup_buf)
         )
@@ -200,10 +201,16 @@
         state[blk] = jnp.concatenate(
             [own_state, jnp.zeros((elements, LANES - quarter), jnp.float32)], axis=1
         ).astype(jnp.bfloat16)
-        for slot in range(1, slots):
-            for k in range(blocks):
-                send(state.at[blk], state.at[slot * blocks + blk], state_sems, away(slot, -1), k)
-        to_siblings(state, state_sems)
+        pending = [(slot, away(slot, -1), k) for slot in range(1, slots) for k in range(blocks)]
+        pending += [(0, dom, k) for k in siblings]
+        each = -(-len(pending) // (len(starts) + 1))
+
+        def send_some():
+            for slot, there, k in pending[:each]:
+                send(state.at[blk], state.at[slot * blocks + blk], state_sems, there, k)
+            del pending[:each]
+
+        send_some()
 
         repeated = jnp.concatenate([own_state] * group, axis=1)
         stacked = jnp.concatenate(
@@ -225,6 +232,7 @@
                 left, coupling[first:last].reshape(depth, width),
                 preferred_element_type=jnp.float32,
             )
+            send_some()
         sent[:, :, :width] = turned.reshape(slots, elements, width).astype(jnp.bfloat16)
         for slot in range(1, slots):
             send(sent.at[slot], back.at[slot], back_sems, away(slot, 1), blk)
@@ -267,23 +275,19 @@
             partial += back[slot].astype(jnp.float32)[:, :width]
         coup[blk, :, :width] = partial
         to_siblings(coup, coup_sems)
+        if sweep == SWEEPS - 1:
+            finish(dual_buf, blocks - 1, dual_sem.at[1])
+            dual = dual_buf[0]
+            for k in range(1, blocks):
+                dual += dual_buf[k]
         finish(coup, blocks - 1, coup_sems.at[1])
         coupled = coup[0]
         for k in range(1, blocks):
             coupled += coup[k]
         full = (coupled[:, :width] * full_mask).astype(jnp.bfloat16).astype(jnp.float32)
-        return (base - invert(own_part(full), full)) * mask, full
-
-    to_siblings(dual_buf, dual_sem)
-    adjoint, full = lax.fori_loop(
-        0, SWEEPS, one_sweep, (base, jnp.zeros((elements, width), jnp.float32))
-    )
+        adjoint = (base - invert(own_part(full), full)) * mask
 
     result_out[:elements, :quarter] = adjoint
-    finish(dual_buf, blocks - 1, dual_sem.at[1])
-    dual = dual_buf[0]
-    for k in range(1, blocks):
-        dual += dual_buf[k]
     weights = dual[:, width:width + 1] - jnp.sum(dual[:, :width] * full, axis=1, keepdims=True)
     lane = lax.broadcasted_iota(jnp.int32, (elements, LANES), 1)
     sub = lax.broadcasted_iota(jnp.int32, (elements, LANES), 0)

time: 30.6 us -> 31.7 us (1.036)
  Pallas kernels: 29.8 us -> 30.9 us
    pallas_call x1, Pallas kernels: 28.5 us -> 29.6 us  [local(): pl.pallas_call(functools.partial(kernel, parts, blocks), out_shape=jax.Sh...]
where the time goes in v6:
time: 31.7 us; the launch traced here: 31.5 us
  Pallas kernels  30.9 us (97%)
  between operations  0.64 us (2%)
    pallas_call x1, Pallas kernels, local(): pl.pallas_call(functools.partial(kernel, parts, blocks), out_shape=jax.Sh...  29.6 us
    pallas_call x1, Pallas kernels, local(): pl.pallas_call(split_result, out_shape=(jax.ShapeDtypeStruct((elements, q...  1.29 us

profile of v6, /device:TPU:0, one launch (start us, length us, event | category | flops | bytes accessed | tf_op | source)
XLA Modules:
  0.0 31.5 jit_solution(9173503483000322967)
XLA Ops:
  0.6 29.6 %shard_map.104.result = f32[16,128]{1,0:T(8,128)} custom-call(s32[8]{0:T(128)} %degree_hbm.1, s32[32]{0:T(128)} %elem_hbm.1, s32[32]{0:T(128)} %side_hbm.1, s32[32]{0:T(128)} %peer_hbm.1, bf16[32,80,320]{2,1,0:T(8,128)(2,1)} %coupling_hbm.1, f32[8,80]{1,0:T(8,128)} %diag_hbm.1, bf16[8,80,320]{2,1,0:T(8,128)(2,1)} %inv_off_hbm.1, f32[8,80]{1,0:T(8,128)} %source_hbm.1, ...), custom_call_target="tpu_custom_call" | custom-call | tf_op jit(solution)/shard_map/pallas_call | solution.py:324
  30.2 1.3 %shard_map.105 = (f32[8,80]{1,0:T(8,128)}, f32[1,8]{1,0:T(1,128)}) custom-call(f32[16,128]{1,0:T(8,128)} %shard_map.104.result), custom_call_target="tpu_custom_call" | custom-call | tf_op jit(solution)/shard_map/pallas_call | solution.py:345

commit v7 on v5

--- a/solution.py
+++ b/solution.py
@@ -45,6 +45,21 @@
     dom = lax.axis_index("dom")
     blk = lax.axis_index("blk")
 
+    siblings = [lax.rem(blk + step, blocks) for step in range(1, blocks)]
+
+    def away(slot, sign):
+        return lax.rem(dom + (sign * unique[slot]) % parts, parts)
+
+    far_first = sorted(range(1, slots), key=lambda slot: -min(unique[slot], parts - unique[slot]))
+    barrier = pltpu.get_barrier_semaphore()
+    for slot in far_first:
+        for k in range(blocks):
+            pl.semaphore_signal(
+                barrier, inc=1, device_id=(away(slot, 1), k), device_id_type=MESH
+            )
+    for k in siblings:
+        pl.semaphore_signal(barrier, inc=1, device_id=(dom, k), device_id_type=MESH)
+
     loads = [
         pltpu.make_async_copy(src, dst, load_sem.at[place])
         for place, (src, dst) in enumerate([
@@ -55,20 +70,6 @@
     ]
     for load in loads:
         load.start()
-
-    siblings = [lax.rem(blk + step, blocks) for step in range(1, blocks)]
-
-    def away(slot, sign):
-        return lax.rem(dom + (sign * unique[slot]) % parts, parts)
-
-    barrier = pltpu.get_barrier_semaphore()
-    for slot in range(1, slots):
-        for k in range(blocks):
-            pl.semaphore_signal(
-                barrier, inc=1, device_id=(away(slot, 1), k), device_id_type=MESH
-            )
-    for k in siblings:
-        pl.semaphore_signal(barrier, inc=1, device_id=(dom, k), device_id_type=MESH)
 
     def send(src, dst, sems, there, k):
         pltpu.make_async_remote_copy(
@@ -152,6 +153,7 @@
         place_of.append(hot)
     place_of = jnp.concatenate(place_of, axis=0).astype(jnp.bfloat16)
     group_col = lax.broadcasted_iota(jnp.int32, (elements, group * quarter), 1)
+    table_lane = lax.broadcasted_iota(jnp.int32, (table, LANES), 1)
     chunk = math.gcd(faces, max(1, LANES // elements))
     chunk_lane = lax.broadcasted_iota(jnp.int32, (quarter, chunk * elements), 1)
     fold_row = lax.broadcasted_iota(jnp.int32, (elements, 2 * chunk * elements), 0)
@@ -197,10 +199,16 @@
             sems.at[sweep] for sems in (state_sem, back_sem, coup_sem)
         )
         own_state = adjoint.astype(jnp.bfloat16).astype(jnp.float32)
-        state[blk] = jnp.concatenate(
+        block = jnp.concatenate(
             [own_state, jnp.zeros((elements, LANES - quarter), jnp.float32)], axis=1
-        ).astype(jnp.bfloat16)
-        for slot in range(1, slots):
+        )
+        turned_block = block
+        for k in range(1, blocks):
+            turned_block = jnp.where(
+                blk == k, pltpu.roll(block, k * quarter % LANES, 1), turned_block
+            )
+        state[blk] = turned_block.astype(jnp.bfloat16)
+        for slot in far_first:
             for k in range(blocks):
                 send(state.at[blk], state.at[slot * blocks + blk], state_sems, away(slot, -1), k)
         to_siblings(state, state_sems)
@@ -226,23 +234,25 @@
                 preferred_element_type=jnp.float32,
             )
         sent[:, :, :width] = turned.reshape(slots, elements, width).astype(jnp.bfloat16)
-        for slot in range(1, slots):
+        for slot in far_first:
             send(sent.at[slot], back.at[slot], back_sems, away(slot, 1), blk)
 
         finish(state, slots * blocks - 1, state_sems.at[1])
-        every = jnp.concatenate(
-            [
-                jnp.concatenate(
-                    [
-                        state[slot * blocks + k].astype(jnp.float32)[:, :quarter]
-                        for k in range(blocks)
-                    ],
-                    axis=1,
-                )
-                for slot in range(slots)
-            ],
-            axis=0,
-        ).astype(jnp.bfloat16)
+        columns = [
+            jnp.concatenate(
+                [state[slot * blocks + k].astype(jnp.float32) for slot in range(slots)], axis=0
+            )
+            for k in range(blocks)
+        ]
+        tiles = []
+        for start in range(0, width, LANES):
+            inside = [k for k in range(blocks)
+                      if k * quarter < start + LANES and (k + 1) * quarter > start]
+            joint = columns[inside[-1]]
+            for k in inside[-2::-1]:
+                joint = jnp.where(table_lane < (k + 1) * quarter - start, columns[k], joint)
+            tiles.append(joint)
+        every = jnp.concatenate(tiles, axis=1)[:, :width].astype(jnp.bfloat16)
         picked = jnp.dot(pick, every, preferred_element_type=jnp.float32).astype(jnp.bfloat16)
         held = jnp.zeros((quarter, chunk * elements), jnp.float32)
         for first in range(0, faces, chunk):

time: 30.6 us -> 31.5 us (1.029)
  Pallas kernels: 29.8 us -> 30.6 us
    pallas_call x1, Pallas kernels: 28.5 us -> 29.3 us  [local(): pl.pallas_call(functools.partial(kernel, parts, blocks), out_shape=jax.Sh...]
where the time goes in v7:
time: 31.5 us; the launch traced here: 31.3 us
  Pallas kernels  30.6 us (97%)
  between operations  0.64 us (2%)
    pallas_call x1, Pallas kernels, local(): pl.pallas_call(functools.partial(kernel, parts, blocks), out_shape=jax.Sh...  29.3 us
    pallas_call x1, Pallas kernels, local(): pl.pallas_call(split_result, out_shape=(jax.ShapeDtypeStruct((elements, q...  1.29 us

profile of v7, /device:TPU:0, one launch (start us, length us, event | category | flops | bytes accessed | tf_op | source)
XLA Modules:
  0.0 31.3 jit_solution(15672557994383590078)
XLA Ops:
  0.6 29.3 %shard_map.104.result = f32[16,128]{1,0:T(8,128)} custom-call(s32[8]{0:T(128)} %degree_hbm.1, s32[32]{0:T(128)} %elem_hbm.1, s32[32]{0:T(128)} %side_hbm.1, s32[32]{0:T(128)} %peer_hbm.1, bf16[32,80,320]{2,1,0:T(8,128)(2,1)} %coupling_hbm.1, f32[8,80]{1,0:T(8,128)} %diag_hbm.1, bf16[8,80,320]{2,1,0:T(8,128)(2,1)} %inv_off_hbm.1, f32[8,80]{1,0:T(8,128)} %source_hbm.1, ...), custom_call_target="tpu_custom_call" | custom-call | tf_op jit(solution)/shard_map/pallas_call | solution.py:330
  30.0 1.3 %shard_map.105 = (f32[8,80]{1,0:T(8,128)}, f32[1,8]{1,0:T(1,128)}) custom-call(f32[16,128]{1,0:T(8,128)} %shard_map.104.result), custom_call_target="tpu_custom_call" | custom-call | tf_op jit(solution)/shard_map/pallas_call | solution.py:351

commit v8 on v7

--- a/solution.py
+++ b/solution.py
@@ -45,21 +45,6 @@
     dom = lax.axis_index("dom")
     blk = lax.axis_index("blk")
 
-    siblings = [lax.rem(blk + step, blocks) for step in range(1, blocks)]
-
-    def away(slot, sign):
-        return lax.rem(dom + (sign * unique[slot]) % parts, parts)
-
-    far_first = sorted(range(1, slots), key=lambda slot: -min(unique[slot], parts - unique[slot]))
-    barrier = pltpu.get_barrier_semaphore()
-    for slot in far_first:
-        for k in range(blocks):
-            pl.semaphore_signal(
-                barrier, inc=1, device_id=(away(slot, 1), k), device_id_type=MESH
-            )
-    for k in siblings:
-        pl.semaphore_signal(barrier, inc=1, device_id=(dom, k), device_id_type=MESH)
-
     loads = [
         pltpu.make_async_copy(src, dst, load_sem.at[place])
         for place, (src, dst) in enumerate([
@@ -70,6 +55,21 @@
     ]
     for load in loads:
         load.start()
+
+    siblings = [lax.rem(blk + step, blocks) for step in range(1, blocks)]
+
+    def away(slot, sign):
+        return lax.rem(dom + (sign * unique[slot]) % parts, parts)
+
+    far_first = sorted(range(1, slots), key=lambda slot: -min(unique[slot], parts - unique[slot]))
+    barrier = pltpu.get_barrier_semaphore()
+    for slot in far_first:
+        for k in range(blocks):
+            pl.semaphore_signal(
+                barrier, inc=1, device_id=(away(slot, 1), k), device_id_type=MESH
+            )
+    for k in siblings:
+        pl.semaphore_signal(barrier, inc=1, device_id=(dom, k), device_id_type=MESH)
 
     def send(src, dst, sems, there, k):
         pltpu.make_async_remote_copy(

time: 31.5 us -> 31.5 us (level)
  no operation moved by 1% of the time
where the time goes in v8:
time: 31.5 us; the launch traced here: 31.3 us
  Pallas kernels  30.6 us (97%)
  between operations  0.64 us (2%)
    pallas_call x1, Pallas kernels, local(): pl.pallas_call(functools.partial(kernel, parts, blocks), out_shape=jax.Sh...  29.3 us
    pallas_call x1, Pallas kernels, local(): pl.pallas_call(split_result, out_shape=(jax.ShapeDtypeStruct((elements, q...  1.29 us

profile of v8, /device:TPU:0, one launch (start us, length us, event | category | flops | bytes accessed | tf_op | source)
XLA Modules:
  0.0 31.3 jit_solution(12846929343989918544)
XLA Ops:
  0.6 29.3 %shard_map.104.result = f32[16,128]{1,0:T(8,128)} custom-call(s32[8]{0:T(128)} %degree_hbm.1, s32[32]{0:T(128)} %elem_hbm.1, s32[32]{0:T(128)} %side_hbm.1, s32[32]{0:T(128)} %peer_hbm.1, bf16[32,80,320]{2,1,0:T(8,128)(2,1)} %coupling_hbm.1, f32[8,80]{1,0:T(8,128)} %diag_hbm.1, bf16[8,80,320]{2,1,0:T(8,128)(2,1)} %inv_off_hbm.1, f32[8,80]{1,0:T(8,128)} %source_hbm.1, ...), custom_call_target="tpu_custom_call" | custom-call | tf_op jit(solution)/shard_map/pallas_call | solution.py:330
  30.0 1.3 %shard_map.105 = (f32[8,80]{1,0:T(8,128)}, f32[1,8]{1,0:T(1,128)}) custom-call(f32[16,128]{1,0:T(8,128)} %shard_map.104.result), custom_call_target="tpu_custom_call" | custom-call | tf_op jit(solution)/shard_map/pallas_call | solution.py:351

commit v9 on v5

--- a/solution.py
+++ b/solution.py
@@ -183,9 +183,6 @@
 
     finish(src_buf, blocks - 1, src_sem.at[1])
     base = invert(src_half, joined(src_buf, elements)) * mask
-    dual_buf[blk, :, width:] = jnp.broadcast_to(
-        jnp.sum(weight * base, axis=1, keepdims=True), (elements, dual_buf.shape[2] - width)
-    )
     loads[8].wait()
 
     def one_sweep(sweep, carry):
@@ -228,6 +225,14 @@
         sent[:, :, :width] = turned.reshape(slots, elements, width).astype(jnp.bfloat16)
         for slot in range(1, slots):
             send(sent.at[slot], back.at[slot], back_sems, away(slot, 1), blk)
+
+        @pl.when(sweep == 0)
+        def send_dual():
+            dual_buf[blk, :, width:] = jnp.broadcast_to(
+                jnp.sum(weight * base, axis=1, keepdims=True),
+                (elements, dual_buf.shape[2] - width),
+            )
+            to_siblings(dual_buf, dual_sem)
 
         finish(state, slots * blocks - 1, state_sems.at[1])
         every = jnp.concatenate(
@@ -274,7 +279,6 @@
         full = (coupled[:, :width] * full_mask).astype(jnp.bfloat16).astype(jnp.float32)
         return (base - invert(own_part(full), full)) * mask, full
 
-    to_siblings(dual_buf, dual_sem)
     adjoint, full = lax.fori_loop(
         0, SWEEPS, one_sweep, (base, jnp.zeros((elements, width), jnp.float32))
     )

time: 30.6 us -> 30.5 us (level)
  no operation moved by 1% of the time
where the time goes in v9:
time: 30.5 us; the launch traced here: 30.3 us
  Pallas kernels  29.7 us (97%)
  between operations  0.64 us (2%)
    pallas_call x1, Pallas kernels, local(): pl.pallas_call(functools.partial(kernel, parts, blocks), out_shape=jax.Sh...  28.4 us
    pallas_call x1, Pallas kernels, local(): pl.pallas_call(split_result, out_shape=(jax.ShapeDtypeStruct((elements, q...  1.29 us

profile of v9, /device:TPU:0, one launch (start us, length us, event | category | flops | bytes accessed | tf_op | source)
XLA Modules:
  0.0 30.3 jit_solution(18076594192270688497)
XLA Ops:
  0.6 28.4 %shard_map.104.result = f32[16,128]{1,0:T(8,128)} custom-call(s32[8]{0:T(128)} %degree_hbm.1, s32[32]{0:T(128)} %elem_hbm.1, s32[32]{0:T(128)} %side_hbm.1, s32[32]{0:T(128)} %peer_hbm.1, bf16[32,80,320]{2,1,0:T(8,128)(2,1)} %coupling_hbm.1, f32[8,80]{1,0:T(8,128)} %diag_hbm.1, bf16[8,80,320]{2,1,0:T(8,128)(2,1)} %inv_off_hbm.1, f32[8,80]{1,0:T(8,128)} %source_hbm.1, ...), custom_call_target="tpu_custom_call" | custom-call | tf_op jit(solution)/shard_map/pallas_call | solution.py:324
  29.0 1.3 %shard_map.105 = (f32[8,80]{1,0:T(8,128)}, f32[1,8]{1,0:T(1,128)}) custom-call(f32[16,128]{1,0:T(8,128)} %shard_map.104.result), custom_call_target="tpu_custom_call" | custom-call | tf_op jit(solution)/shard_map/pallas_call | solution.py:345
